TPU v7x, 32 devices: a whole 2x2x4 slice. The times are simulated.
32 devices in a mesh: dp: 4 (over y, x), gx: 2 (over core), yz: 4 (over z).
Axes of the slice: x: 2, y: 2, z: 4, core: 2. Of those that a mesh axis runs over, the one named last changes fastest.
Arguments:
- volumes: bfloat16 [4, 4, 2, 4, 16384], P('dp', None, 'gx', 'yz'), may hold values from -6 to 6
- first_kernel: bfloat16 [32, 4, 3, 3, 3], replicated, may hold values from -0.625 to 0.625
- second_kernel: bfloat16 [64, 32, 3, 3, 3], replicated, may hold values from -0.21875 to 0.21875
- cotangent: bfloat16 [4, 64, 2, 4, 256], P('dp', None, 'gx', 'yz'), may hold values from -6 to 6
Outputs:
- features: bfloat16 [4, 64, 2, 4, 256], P('dp', None, 'gx', 'yz')
- act_grad: float32 [4, 32, 2, 4, 2048], P('dp', None, 'gx', 'yz')
- first_grad: float32 [32, 4, 3, 3, 3], replicated
- second_grad: float32 [64, 32, 3, 3, 3], replicated
All inputs are finite; a program needn't handle non-finite values.
Results may differ from a plain program's by a relative error of at most 0.019.
The roundings to bfloat16 on the way count: a program that leaves them out, or rounds other values in their place, can miss the bound.
Values may be sent and summed in bfloat16 or wider, within the bound.
No kernel may reach another device: no remote copies, remote signals or barrier semaphores. Data moves between devices by JAX's collectives and lax.ppermute only.
A program may use at most 128 MiB of HBM per device.

v0:
```python
import functools

import jax
import jax.numpy as jnp
from jax import lax
from jax.experimental import pallas as pl
from jax.experimental.pallas import tpu as pltpu
from jax.sharding import PartitionSpec as P

CX = 32
CY = 32
CZ = 16
SLOPE = 0.3
F32 = jnp.float32
BF16 = jnp.bfloat16


def leaky(values):
    return jnp.maximum(values, SLOPE * values)


def leaky_slope(values):
    return jnp.where(values > 0, jnp.float32(1.0), jnp.float32(SLOPE))


def convolve_valid(padded, kernel):
    return lax.conv_general_dilated(
        padded,
        kernel,
        (1, 1, 1),
        "VALID",
        dimension_numbers=("NCDHW", "OIDHW", "NCDHW"),
        preferred_element_type=F32,
    )


def kernel_grad(padded, grad):
    result = lax.conv_general_dilated(
        padded,
        grad,
        (1, 1, 1),
        "VALID",
        dimension_numbers=("CNDHW", "IODHW", "NCDHW"),
        preferred_element_type=F32,
    )
    return result.transpose(1, 0, 2, 3, 4)


def average_pool(values):
    bat, chan, xs, ys, zs = values.shape
    return values.reshape(bat, chan, xs // 2, 2, ys // 2, 2, zs // 2, 2).mean(axis=(3, 5, 7))


def spread_back(values):
    bat, chan, xs, ys, zs = values.shape
    grown = jnp.broadcast_to(
        values[:, :, :, None, :, None, :, None], (bat, chan, xs, 2, ys, 2, zs, 2)
    )
    return grown.reshape(bat, chan, 2 * xs, 2 * ys, 2 * zs) * 0.125


def unflatten(values, factor):
    return values[:, :, 0, 0].reshape(
        values.shape[0], values.shape[1], CX // factor, CY // factor, CZ // factor
    )


def flatten(values):
    return values.reshape(values.shape[0], values.shape[1], 1, 1, -1)


def extend_along(values, dim, axis, routes):
    size = values.shape[dim]
    first = lax.slice_in_dim(values, 0, 1, axis=dim)
    last = lax.slice_in_dim(values, size - 1, size, axis=dim)
    before = lax.ppermute(last, axis, routes)
    after = lax.ppermute(first, axis, [(b, a) for a, b in routes])
    return jnp.concatenate([before, values, after], axis=dim)


def extend(values, rows_y, rows_z):
    planes = lax.axis_size("gx")
    count = rows_y * rows_z
    values = extend_along(values, 2, "gx", [(i, i + 1) for i in range(planes - 1)])
    values = extend_along(values, 3, "yz", [(i, i + rows_z) for i in range(count - rows_z)])
    return extend_along(
        values, 4, "yz", [(i, i + 1) for i in range(count - 1) if (i + 1) % rows_z]
    )


def on_device_plain(rows_y, rows_z, volumes, first_kernel, second_kernel, cotangent):
    upstream = unflatten(cotangent, 4)
    padded_in = extend(unflatten(volumes, 1), rows_y, rows_z)
    pre_first = convolve_valid(padded_in, first_kernel)
    act_first = average_pool(leaky(pre_first)).astype(BF16)
    padded_mid = extend(act_first, rows_y, rows_z)
    pre_second = convolve_valid(padded_mid, second_kernel)
    features = average_pool(leaky(pre_second)).astype(BF16)
    grad_second = (spread_back(upstream.astype(F32)) * leaky_slope(pre_second)).astype(BF16)
    flipped = jnp.flip(second_kernel, (2, 3, 4)).transpose(1, 0, 2, 3, 4)
    act_grad = convolve_valid(extend(grad_second, rows_y, rows_z), flipped)
    grad_first = (spread_back(act_grad) * leaky_slope(pre_first)).astype(BF16)
    first_grad, second_grad = lax.psum(
        (kernel_grad(padded_in, grad_first), kernel_grad(padded_mid, grad_second)),
        ("dp", "gx", "yz"),
    )
    return (flatten(features), flatten(act_grad), first_grad, second_grad)


FINE = 48 * CZ
KEPT = 40 * CZ
OWN = CY * CZ
COARSE = 256
MID = (CY // 2) * (CZ // 2)
NF = 18
NS = 17


def grid(shape):
    return [lax.broadcasted_iota(jnp.int32, shape, dim) for dim in range(2)]


def one_where(condition, value=1.0):
    return jnp.where(condition, value, 0.0).astype(BF16)


def fine_to_mid(lane):
    return (lane >> 5) * 8 + ((lane & 15) >> 1) + jnp.where(lane >= OWN + 64, 96, 0)


def rim_table():
    row, lane = grid((256, 256))
    edge = jnp.where(lane < 128, 0, 7)
    place = (row >> 5) * 4 + (row & 3)
    return one_where(jnp.logical_and(((row >> 2) & 7) == edge, place == (lane & 127)))


def pool_first_table():
    row, lane = grid((KEPT, COARSE))
    place = jnp.where((row & 17) == 0, fine_to_mid(row), -1)
    return one_where(place == lane, 0.125)


def spread_first_table():
    row, lane = grid((MID, OWN))
    return one_where(fine_to_mid(lane) == row, 0.125)


def pool_second_table():
    row, lane = grid((MID, 128))
    place = jnp.where((row & 9) == 0, (row >> 4) * 4 + ((row & 7) >> 1), -1)
    return one_where(place == lane, 0.125)


def spread_second_table():
    row, lane = grid((128, COARSE))
    place = jnp.where(lane < MID, (lane >> 4) * 4, jnp.where(lane < 192, 32, 36))
    place = place + ((lane & 7) >> 1)
    used = jnp.logical_or(lane < MID + 8, lane >= COARSE - 8)
    return one_where(jnp.logical_and(used, place == row), 0.125)


def fold_rows(values):
    lane = grid((16, 128))[1]
    kept = [
        jnp.where(lane < 32, values[16 * q : 16 * q + 16], jnp.zeros((16, 128), F32))
        for q in range(4)
    ]
    return kept[0] + sum(pltpu.roll(kept[q], 32 * q, 1) for q in range(1, 4))


def unfold_rows(values):
    parts = [values] + [pltpu.roll(values, 128 - 32 * q, 1) for q in range(1, 4)]
    return jnp.concatenate(parts, axis=0)


def dot(a, b):
    return jnp.dot(a, b, preferred_element_type=F32)


def dot_lanes(a, b):
    return lax.dot_general(a, b, (((1,), (1,)), ((), ())), preferred_element_type=F32)


def pack_kernel(vol_ref, cot_ref, own_ref, x_ref, near_ref, far_ref, xnear_ref, xfar_ref):
    gx = lax.axis_index("gx")
    odd = lax.axis_index("yz") % 2
    own_ref[0:8, :] = jnp.zeros((8, OWN), F32)
    own_ref[128:136, :] = jnp.zeros((8, OWN), F32)
    for x in range(CX):
        own_ref[4 + 4 * x : 8 + 4 * x, :] = vol_ref[:, x * OWN : (x + 1) * OWN].astype(F32)
    start = pl.multiple_of(112 * (1 - gx), 8)
    blank = jnp.zeros((8, OWN), F32)
    face = jnp.concatenate([own_ref[pl.ds(start, 24), :], blank])
    x_ref[0:32, :] = face.astype(BF16)
    cot = cot_ref[...]
    wide = cot.astype(F32)
    first = gx == 0
    end = jnp.where(first, pltpu.roll(wide[:, 128:256], 32, 1), wide[:, 0:128])
    x_ref[32:48, 0:128] = fold_rows(end).astype(BF16)
    x_ref[32:48, 128:OWN] = jnp.zeros((16, OWN - 128), BF16)
    rims = dot(cot, rim_table())
    for low, side_ref, xside_ref in ((odd, near_ref, xnear_ref), (1 - odd, far_ref, xfar_ref)):
        lanes = pl.ds(pl.multiple_of((OWN - 128) * (1 - low), 128), 128)
        tail = jnp.concatenate([own_ref[128:136, lanes], blank[:, 0:128]])
        side_ref[0:128, :] = own_ref[0:128, lanes].astype(BF16)
        side_ref[128:144, :] = tail.astype(BF16)
        edge = jnp.concatenate([own_ref[pl.ds(start, 24), lanes], blank[:, 0:128]])
        xside_ref[0:32, :] = edge.astype(BF16)
        rim = jnp.where(low == 1, rims[:, 0:128], rims[:, 128:256])
        side_ref[144:160, :] = fold_rows(rim).astype(BF16)
        corner = jnp.where(first, pltpu.roll(rim, 100, 1), rim)
        xside_ref[32:48, :] = fold_rows(corner).astype(BF16)


def prepare_kernel(
    after_ref,
    k1_ref,
    k2_ref,
    w1_ref,
    w2_ref,
    w3_ref,
    pool_first_ref,
    spread_first_ref,
    pool_second_ref,
    spread_second_ref,
    w1_rows,
):
    del after_ref
    pool_first_ref[...] = pool_first_table()
    spread_first_ref[...] = spread_first_table()
    pool_second_ref[...] = pool_second_table()
    spread_second_ref[...] = spread_second_table()
    w1_rows[...] = jnp.zeros_like(w1_rows)
    for dx in range(3):
        for at in range(9):
            block = k1_ref[dx * 9 + at].astype(F32)
            for k in range(2):
                row = at * 16 + 4 * (dx + k)
                w1_rows[row : row + 4, 32 * k : 32 * k + 32] = block
    w1_ref[...] = w1_rows[...].T.astype(BF16)
    k2 = k2_ref[...].astype(F32)
    flipped = jnp.concatenate([k2[32 * n : 32 * n + 32] for n in range(26, -1, -1)], axis=1)
    for out_ref, one in ((w2_ref, k2.T), (w3_ref, flipped)):
        high, wide = one.shape
        for r in range(4):
            parts = [jnp.zeros((high, wide // 3 * r), F32)] if r else []
            parts.append(one)
            if r < 3:
                parts.append(jnp.zeros((high, wide // 3 * (3 - r)), F32))
            row = jnp.concatenate(parts, axis=1)
            out_ref[high * r : high * r + high, :] = row.astype(BF16)


def shifted(tile, period, lane):
    size = tile.shape[1]
    z = lane % period
    blank = jnp.zeros_like(tile)
    along = (
        jnp.where(z == 0, blank, pltpu.roll(tile, 1, 1)),
        tile,
        jnp.where(z == period - 1, blank, pltpu.roll(tile, size - 1, 1)),
    )
    return [
        pltpu.roll(moved, shift, 1) if shift else moved
        for shift in (period, 0, size - period)
        for moved in along
    ]


def pooled(values, period):
    blocks = []
    for at in range(0, values.shape[1], 128):
        block = values[:, at : at + 128]
        block = block + pltpu.roll(block, 127, 1)
        blocks.append(block + pltpu.roll(block, 128 - period, 1))
    return jnp.concatenate(blocks, axis=1).astype(BF16)


def split(values):
    top = values.astype(BF16)
    return jnp.concatenate([top, (values - top.astype(F32)).astype(BF16)], axis=0)


def main_kernel(
    rows_y,
    own_ref,
    cot_ref,
    rx_ref,
    rnear_ref,
    rfar_ref,
    rxnear_ref,
    rxfar_ref,
    w1_ref,
    w2_ref,
    w3_ref,
    pool_first_ref,
    spread_first_ref,
    spread_second_ref,
    act_second,
    act_grad_ref,
    kept_ref,
    sent_ref,
    vol,
    cols_first,
    pre_first,
    pooled_first,
    cols_second,
    spread_up,
    grad_own,
    cols_grad,
    half_grad,
    grads_ref,
    sums_ref,
):
    gx = lax.axis_index("gx")
    block_y = lax.axis_index("yz")

    odd = block_y % 2 == 1
    inner = jnp.logical_and(block_y > 0, block_y < rows_y - 1)

    def above_below(near, far):
        near, far = near.astype(F32), far.astype(F32)
        far = jnp.where(inner, far, jnp.zeros_like(far))
        return jnp.where(odd, far, near), jnp.where(odd, near, far)

    vol[...] = jnp.zeros_like(vol)
    up, down = above_below(rnear_ref[0:144, :], rfar_ref[0:144, :])
    vol[pl.ds(2 * gx, 17), :, OWN : OWN + 128] = up[0:136].reshape(17, 8, 128)
    vol[pl.ds(2 * gx, 17), :, OWN + 128 : FINE] = down[0:136].reshape(17, 8, 128)
    vol[pl.ds(2 * gx, 17), :, 0:OWN] = own_ref[...]
    end = pl.ds(16 * (1 - gx), 3)
    vol[end, :, 0:OWN] += rx_ref[0:32, :].astype(F32)[0:24].reshape(3, 8, OWN)
    up, down = above_below(rxnear_ref[0:32, :], rxfar_ref[0:32, :])
    vol[end, :, OWN : OWN + 128] += up[0:24].reshape(3, 8, 128)
    vol[end, :, OWN + 128 : FINE] += down[0:24].reshape(3, 8, 128)

    slot = grid((64, 128))[1]

    def upstream(plane, up, down):
        return jnp.where(slot < 32, plane, jnp.where(slot < 36, up, down)).astype(BF16)

    def moved_to(values, lane_from, lane_to):
        shift = (lane_to - lane_from) % 128
        return pltpu.roll(values, shift, 1) if shift else values

    cot = cot_ref[...].astype(F32)
    up, down = above_below(rnear_ref[144:160, :], rfar_ref[144:160, :])
    up, down = unfold_rows(up), unfold_rows(down)
    planes = [
        upstream(
            moved_to(cot[:, p // 4 * 128 : p // 4 * 128 + 128], p % 4 * 32, 0),
            moved_to(up, 4 * p, 32),
            moved_to(down, 4 * p, 36),
        )
        for p in range(8)
    ]
    up, down = above_below(rxnear_ref[32:48, :], rxfar_ref[32:48, :])
    planes.append(
        upstream(
            unfold_rows(rx_ref[32:48, 0:128].astype(F32)),
            moved_to(unfold_rows(up), 0, 32),
            moved_to(unfold_rows(down), 0, 36),
        )
    )
    spread = dot(jnp.concatenate(planes, axis=0), spread_second_ref[...])
    for p in range(8):
        spread_up[p + gx] = spread[64 * p : 64 * p + 64]
    spread_up[8 * (1 - gx)] = spread[512:576]

    lane_fine = lax.broadcasted_iota(jnp.int32, (16, FINE), 1)
    near = lax.broadcasted_iota(jnp.int32, (16, 128), 1) < 64

    def first_layer(j):
        tile = jnp.concatenate([vol[j], vol[j + 1]], axis=0).astype(BF16)
        parts = []
        for moved in shifted(tile, CZ, lane_fine):
            edge = jnp.where(near, moved[:, OWN : OWN + 128], moved[:, OWN + 128 : FINE])
            parts.append(jnp.concatenate([moved[:, 0:OWN], edge], axis=1))
        cols = jnp.concatenate(parts, axis=0)
        cols_first[j] = cols[:, 0:OWN]
        pre = dot(w1_ref[...], cols)
        pre_first[j] = pre[:, 0:OWN]
        sloped = leaky(pre)
        pooled_first[j] = pooled(sloped[0:32] + sloped[32:64], CZ)

    lane = lax.broadcasted_iota(jnp.int32, (32, COARSE), 1)
    valid = jnp.logical_or(
        lane < MID,
        jnp.logical_or(
            jnp.logical_and(lane < 192, block_y < rows_y - 1),
            jnp.logical_and(lane >= 192, block_y > 0),
        ),
    )

    def columns_second(step):
        six = pooled_first[6 * step : 6 * step + 6].reshape(192, KEPT)
        picked = dot(six, pool_first_ref[...])
        for k in range(6):
            plane = jnp.where(valid, picked[k * 32 : k * 32 + 32], 0.0).astype(BF16)
            parts = shifted(plane, CZ // 2, lane)
            cols_second[6 * step + k + 1] = jnp.concatenate(parts, axis=0)

    lane_grad = lax.broadcasted_iota(jnp.int32, (64, COARSE), 1)

    def second_layer(k, pre):
        act_second[k] = leaky(pre[:, 0:MID])
        given = spread_up[(k + gx) // 2]
        rounded = jnp.where(pre > 0, given, SLOPE * given).astype(BF16)
        parts = [moved[:, 0:MID] for moved in shifted(rounded, CZ // 2, lane_grad)]
        cols_grad[k + 1] = jnp.concatenate(parts, axis=0)
        kept = rounded[:, 0:MID]
        if k == 0:
            kept = jnp.where(gx == 0, kept, jnp.zeros_like(kept))
        if k == NS - 1:
            kept = jnp.where(gx == 1, kept, jnp.zeros_like(kept))
        grad_own[k + 2 - gx] = kept

    def four_second(k):
        four = dot(w2_ref[...], cols_second[pl.ds(k + gx, 6)].reshape(1728, COARSE))
        for r in range(4):
            second_layer(k + r, four[64 * r : 64 * r + 64])

    def eight_back(base):
        cols = jnp.concatenate(
            [
                cols_grad[pl.ds(base + gx, 6)].reshape(3456, MID),
                cols_grad[pl.ds(base + 4 + gx, 6)].reshape(3456, MID),
            ],
            axis=1,
        )
        back = dot(w3_ref[...], cols)
        for m in range(8):
            row, lanes = 32 * (m % 4), MID * (m // 4)
            plane = back[row : row + 32, lanes : lanes + MID]
            act_grad_ref[:, base + m, :] = plane
            half_grad[base + m] = split(plane)

    def four_first(step):
        spread = dot(
            half_grad[4 * step : 4 * step + 4].reshape(256, MID), spread_first_ref[...]
        )
        backs = []
        for k in range(4):
            whole = spread[k * 64 : k * 64 + 32] + spread[k * 64 + 32 : k * 64 + 64]
            less = SLOPE * whole
            pre = pre_first[4 * step + k + 2 * gx]
            parts = [jnp.where(pre[r : r + 32] > 0, whole, less) for r in (0, 32)]
            backs.append(jnp.concatenate(parts, axis=0).astype(BF16))
        cols = [cols_first[4 * step + k + 2 * gx] for k in range(4)]
        return dot_lanes(jnp.concatenate(cols, axis=1), jnp.concatenate(backs, axis=1))

    cols_second[0] = jnp.zeros((288, COARSE), BF16)
    cols_second[NF + 1] = jnp.zeros((288, COARSE), BF16)
    cols_grad[0] = jnp.zeros((576, MID), BF16)
    cols_grad[NS + 1] = jnp.zeros((576, MID), BF16)
    for k in (0, 1, 18, 19):
        grad_own[k] = jnp.zeros((64, MID), BF16)

    for step in range(3):
        for j in range(6 * step, 6 * step + 6):
            first_layer(j)
        columns_second(step)
        four_second(4 * step)
    eight_back(0)
    four_second(12)
    last = cols_second[pl.ds(NS - 1 + gx, 3)].reshape(864, COARSE)
    second_layer(NS - 1, dot(w2_ref[0:64, 0:864], last))
    first = four_first(0) + four_first(1)
    eight_back(8)
    left = jnp.concatenate([cols_second[q + 2 * gx][:, 0:MID] for q in range(18)], axis=1)
    right = jnp.concatenate([grad_own[q : q + 3].reshape(192, MID) for q in range(18)], axis=1)
    grads_ref[:, 0:192] = dot_lanes(left, right)
    first = first + four_first(2) + four_first(3)
    grads_ref[0:144, 192:256] = first

    both = pltpu.roll(grads_ref[0:144, 128:256], 64, 1)
    sums_ref[...] = both + pltpu.roll(pltpu.roll(both, 96, 1), 140, 0)
    slot = grid((72, 128))[1]
    place = grid((24, 128))[1] // 32

    def folded(half):
        rows = pl.multiple_of(144 * half, 8)
        right = grads_ref[pl.ds(rows, 72), 128:256]
        right_next = pltpu.roll(grads_ref[pl.ds(rows + 72, 72), 128:256], 64, 1)
        parts = [
            sums_ref[pl.ds(pl.multiple_of(72 * half + 24 * q, 8), 24), :] for q in range(3)
        ]
        last = jnp.where(place == 2, pltpu.roll(parts[2], 64, 1), jnp.zeros((24, 128), F32))
        last = jnp.where(place == 1, pltpu.roll(parts[1], 32, 1), last)
        last = jnp.where(place == 0, parts[0], last)
        return [grads_ref[pl.ds(rows, 144), 0:128], jnp.where(slot < 64, right, right_next), last]

    for half_ref, half in ((kept_ref, gx), (sent_ref, 1 - gx)):
        row = 0
        for part in folded(half):
            half_ref[row : row + part.shape[0], :] = part.astype(half_ref.dtype)
            row += part.shape[0]


def features_kernel(act_second_ref, pool_second_ref, features_ref):
    gx = lax.axis_index("gx")
    sums = [
        pooled(act_second_ref[2 * p + gx] + act_second_ref[2 * p + 1 + gx], CZ // 2)
        for p in range(8)
    ]
    picked = dot(jnp.concatenate(sums, axis=0), pool_second_ref[...])
    for half in range(2):
        whole = picked[256 * half : 256 * half + 64]
        for k in range(1, 4):
            block = picked[256 * half + 64 * k : 256 * half + 64 * k + 64]
            whole = whole + pltpu.roll(block, 32 * k, 1)
        features_ref[:, 128 * half : 128 * half + 128] = whole.astype(BF16)


def unpack_kernel(mine_ref, other_ref, second_ref, first_ref):
    first = lax.axis_index("gx") == 0
    mine, other = mine_ref[...].astype(F32), other_ref[...].astype(F32)
    halves = jnp.where(first, mine, other), jnp.where(first, other, mine)
    for h, half in enumerate(halves):
        row = 144 * h
        second_ref[2, row : row + 144] = half[0:144, 0:64]
        second_ref[1, row : row + 144] = half[0:144, 64:128]
        second_ref[0, row : row + 72] = half[144:216, 0:64]
        second_ref[0, row + 72 : row + 144] = half[144:216, 64:128]
    for at in range(9):
        for dx in range(3):
            h, row = divmod(at * 16 + 4 * dx, 72)
            q, row = divmod(row, 24)
            first_ref[dx * 9 + at] = halves[h][216 + row : 220 + row, 32 * q : 32 * q + 32]


def call(kernel, outs, limit, scratch=(), cost=None, in_vmem=False):
    return pl.pallas_call(
        kernel,
        out_shape=[
            pltpu.VMEM(shape, dtype) if in_vmem else jax.ShapeDtypeStruct(shape, dtype)
            for shape, dtype in outs
        ],
        cost_estimate=cost,
        scratch_shapes=[pltpu.VMEM(shape, dtype) for shape, dtype in scratch],
        compiler_params=pltpu.CompilerParams(vmem_limit_bytes=limit * 1024 * 1024),
    )


def in_hbm(values):
    return pltpu.with_memory_space_constraint(values, pltpu.HBM)


def swap_cores(values):
    return lax.ppermute(values, "gx", [(0, 1), (1, 0)])


def sum_of_four(part, axis):
    came = [lax.ppermute(part, axis, [(i, i ^ k) for i in range(4)]) for k in range(1, 4)]
    terms = [term.astype(F32) for term in [part] + came]
    return ((terms[0] + terms[1]) + (terms[2] + terms[3])).astype(BF16)


def on_device_kernels(rows_y, volumes, first_kernel, second_kernel, cotangent):
    cot = cotangent.reshape(64, 256)
    k1 = first_kernel.transpose(2, 3, 4, 1, 0).reshape(27, 4, 32)
    k2 = second_kernel.transpose(2, 3, 4, 1, 0).reshape(864, 64)
    own, x_face, near, far, x_near, x_far = call(
        pack_kernel,
        [
            ((136, OWN), F32),
            ((48, OWN), BF16),
            ((160, 128), BF16),
            ((160, 128), BF16),
            ((48, 128), BF16),
            ((48, 128), BF16),
        ],
        16,
    )(in_hbm(volumes.reshape(4, CX * OWN)), in_hbm(cot))
    *weights, pool_first, spread_first, pool_second, spread_second = call(
        prepare_kernel,
        [
            ((64, 144), BF16),
            ((256, 1728), BF16),
            ((128, 3456), BF16),
            ((KEPT, COARSE), BF16),
            ((MID, OWN), BF16),
            ((MID, 128), BF16),
            ((128, COARSE), BF16),
        ],
        16,
        [((144, 64), F32)],
        pl.CostEstimate(flops=10**8, bytes_accessed=2 * 10**6, transcendentals=0),
    )(x_far, in_hbm(k1), in_hbm(k2))

    def paired(values, partner):
        routes = [
            (g * rows_y + i, partner(g, i)) for g in range(2) for i in range(rows_y)
        ]
        return lax.ppermute(values, ("gx", "yz"), routes)

    def other_side(g, i, across):
        j = i + (1 if i % 2 else -1)
        if 0 <= j < rows_y:
            return (g ^ across) * rows_y + j
        return (1 - g) * rows_y + i

    got_near = lax.ppermute(near, "yz", [(i, i ^ 1) for i in range(rows_y)])
    got_far = paired(far, lambda g, i: other_side(g, i, 0))
    got_x = lax.ppermute(x_face, "gx", [(0, 1), (1, 0)])
    got_x_near = paired(x_near, lambda g, i: (1 - g) * rows_y + (i ^ 1))
    got_x_far = paired(x_far, lambda g, i: other_side(g, i, 1))

    act_second, act_grad, kept, sent = call(
        functools.partial(main_kernel, rows_y),
        [
            ((NS, 64, MID), F32),
            ((32, 16, MID), F32),
            ((240, 128), F32),
            ((240, 128), BF16),
        ],
        32,
        [
            ((19, 8, FINE), F32),
            ((NF, 144, OWN), BF16),
            ((NF, 64, OWN), F32),
            ((NF, 32, KEPT), BF16),
            ((NF + 2, 288, COARSE), BF16),
            ((9, 64, COARSE), F32),
            ((20, 64, MID), BF16),
            ((NS + 2, 576, MID), BF16),
            ((16, 64, MID), BF16),
            ((288, 256), F32),
            ((144, 128), F32),
        ],
        in_vmem=True,
    )(
        own.reshape(17, 8, OWN),
        cot,
        got_x,
        got_near,
        got_far,
        got_x_near,
        got_x_far,
        *weights,
        pool_first,
        spread_first,
        spread_second,
    )
    [features] = call(features_kernel, [((64, 256), BF16)], 8)(act_second, pool_second)
    part = (kept + swap_cores(sent).astype(F32)).astype(BF16)
    part = sum_of_four(part, "dp")
    part, features = lax.optimization_barrier((part, features))
    mine = sum_of_four(part, "yz")
    second, first = call(unpack_kernel, [((3, 288, 64), F32), ((27, 4, 32), F32)], 8)(
        mine, swap_cores(mine)
    )
    return (
        features.reshape(1, 64, 1, 1, 256),
        act_grad.reshape(1, 32, 1, 1, 2048),
        first.reshape(3, 3, 3, 4, 32).transpose(4, 3, 0, 1, 2),
        second.reshape(3, 3, 3, 32, 64).transpose(4, 3, 0, 1, 2),
    )


def solution(mesh):
    placed = (P("dp", None, "gx", "yz", None), P(), P(), P("dp", None, "gx", "yz", None))
    rows_y = min(4, mesh.shape["yz"])
    rows_z = mesh.shape["yz"] // rows_y
    if rows_z == 1 and rows_y == 4 and mesh.shape["gx"] == 2 and mesh.shape["dp"] == 4:
        body = functools.partial(on_device_kernels, rows_y)
    else:
        body = functools.partial(on_device_plain, rows_y, rows_z)
    return jax.shard_map(
        body,
        mesh=mesh,
        in_specs=placed,
        out_specs=(P("dp", None, "gx", "yz", None), P("dp", None, "gx", "yz", None), P(), P()),
        check_vma=False,
    )
```

profile of v0, /device:TPU:0, one launch (start us, length us, event | category | flops | bytes accessed | tf_op | source)
XLA Modules:
  0.0 36.8 jit_solution(17955696350267832567)
XLA Ops:
  0.6 1.3 %shard_map.75 = (f32[136,512]{1,0:T(8,128)S(1)}, bf16[48,512]{1,0:T(8,128)(2,1)S(1)}, bf16[160,128]{1,0:T(8,128)(2,1)S(1)}, bf16[160,128]{1,0:T(8,128)(2,1)S(1)}...) custom-call(bf16[4,16384]{1,0:T(4,128)(2,1)} %bitcast.21, bf16[64,256]{1,0:T(8,128)(2,1)} %bitcast.19), custom_call_target="tpu_custom_call" | custom-call | tf_op jit(solution)/shard_map/pallas_call | solution.py:564
  1.9 0.5 %collective-permute-start = (bf16[48,512]{1,0:T(8,128)(2,1)S(1)}, bf16[48,512]{1,0:T(8,128)(2,1)S(1)}, u32[]{:S(2)}, u32[]{:S(2)}) collective-permute-start(bf16[48,512]{1,0:T(8,128)(2,1)S(1)} %get-tuple-element.26), channel_id=1, source_target_pairs={{0,4},{4,0},{1,5},{5,1},{2,6},{6,2},{3,7},{7,3},{8,12},{12,8},{9,1... | collective-permute-start | bytes 147464 | tf_op jit(solution)/shard_map/ppermute | solution.py:606
  2.4 2.7 %collective-permute-start.1 = (bf16[160,128]{1,0:T(8,128)(2,1)S(1)}, bf16[160,128]{1,0:T(8,128)(2,1)S(1)}, u32[]{:S(2)}, u32[]{:S(2)}) collective-permute-start(bf16[160,128]{1,0:T(8,128)(2,1)S(1)} %get-tuple-element.27), channel_id=1, source_target_pairs={{0,1},{1,0},{2,3},{3,2},{4,5},{5,4},{6,7},{7,6},{8,9},{9,8},{10,11... | collective-permute-start | bytes 122888 | tf_op jit(solution)/shard_map/ppermute | solution.py:604
  5.1 0.2 collective-permute-start.2
  5.2 2.5 %collective-permute-start.3 = (bf16[48,128]{1,0:T(8,128)(2,1)S(1)}, bf16[48,128]{1,0:T(8,128)(2,1)S(1)}, u32[]{:S(2)}, u32[]{:S(2)}) collective-permute-start(bf16[48,128]{1,0:T(8,128)(2,1)S(1)} %get-tuple-element.29), channel_id=1, source_target_pairs={{0,5},{1,4},{2,7},{3,6},{4,1},{5,0},{6,3},{7,2},{8,13},{9,12},{10,... | collective-permute-start | bytes 36872 | tf_op jit(solution)/shard_map/ppermute | solution.py:596
  7.7 0.6 %collective-permute-start.4 = (bf16[48,128]{1,0:T(8,128)(2,1)S(1)}, bf16[48,128]{1,0:T(8,128)(2,1)S(1)}, u32[]{:S(2)}, u32[]{:S(2)}) collective-permute-start(bf16[48,128]{1,0:T(8,128)(2,1)S(1)} %get-tuple-element.30.after_ref), channel_id=1, source_target_pairs={{0,4},{1,6},{2,5},{3,7},{4,0},{5,2},{6,1},{7,3},{8,12},{9,14},{10,... | collective-permute-start | bytes 36872 | tf_op jit(solution)/shard_map/ppermute | solution.py:596
  8.3 1.6 %shard_map.76 = (bf16[64,144]{1,0:T(8,128)(2,1)S(1)}, bf16[256,1728]{1,0:T(8,128)(2,1)S(1)}, bf16[128,3456]{1,0:T(8,128)(2,1)S(1)}, bf16[640,256]{1,0:T(8,128)(2...) custom-call(bf16[48,128]{1,0:T(8,128)(2,1)S(1)} %get-tuple-element.30.after_ref, ...), custom_call_target="tpu_custom_call" | custom-call | flops 100000000 | bytes 2000000 | tf_op jit(solution)/shard_map/pallas_call | solution.py:576
  10.0 8.2 %shard_map.77 = (f32[17,64,128]{2,1,0:T(8,128)S(1)}, f32[32,16,128]{2,1,0:T(8,128)S(1)}, f32[240,128]{1,0:T(8,128)S(1)}, bf16[240,128]{1,0:T(8,128)(2,1)S(1)}) custom-call(f32[17,8,512]{2,1,0:T(8,128)S(1)} %bitcast.18, bf16[64,256]{1,0:T(8,128)(2,1)S(1)} %bitcast.20, bf16[48,512]{1,0:T(8,128)(2,1)S(1)} %collective-permute-done.rx_ref, ...), custom_call_target="tpu_custom_call" | custom-call | tf_op jit(solution)/shard_map/pallas_call | solution.py:610
  18.4 1.2 %collective-permute-done.5 = bf16[240,128]{1,0:T(8,128)(2,1)S(1)} collective-permute-done((bf16[240,128]{1,0:T(8,128)(2,1)S(1)}, bf16[240,128]{1,0:T(8,128)(2,1)S(1)}, u32[]{:S(2)}, u32[]{:S(2)}) %collective-permute-start.5) | collective-permute-done | bytes 61472 | tf_op jit(solution)/shard_map/ppermute | solution.py:551
  19.5 2.5 %collective-permute-start.8 = (bf16[240,128]{1,0:T(8,128)(2,1)S(1)}, bf16[240,128]{1,0:T(8,128)(2,1)S(1)}, u32[]{:S(2)}, u32[]{:S(2)}) collective-permute-start(bf16[240,128]{1,0:T(8,128)(2,1)S(1)} %add_convert_fusion.2), channel_id=1, source_target_pairs={{0,24},{8,16},{16,8},{24,0},{1,25},{9,17},{17,9},{25,1},{2,26},{10... | collective-permute-start | bytes 184328 | tf_op jit(solution)/shard_map/ppermute | solution.py:555
  22.1 0.5 %collective-permute-start.7 = (bf16[240,128]{1,0:T(8,128)(2,1)S(1)}, bf16[240,128]{1,0:T(8,128)(2,1)S(1)}, u32[]{:S(2)}, u32[]{:S(2)}) collective-permute-start(bf16[240,128]{1,0:T(8,128)(2,1)S(1)} %add_convert_fusion.2), channel_id=1, source_target_pairs={{0,16},{8,24},{16,0},{24,8},{1,17},{9,25},{17,1},{25,9},{2,18},{10... | collective-permute-start | bytes 184328 | tf_op jit(solution)/shard_map/ppermute | solution.py:555
  22.6 0.5 %collective-permute-start.6 = (bf16[240,128]{1,0:T(8,128)(2,1)S(1)}, bf16[240,128]{1,0:T(8,128)(2,1)S(1)}, u32[]{:S(2)}, u32[]{:S(2)}) collective-permute-start(bf16[240,128]{1,0:T(8,128)(2,1)S(1)} %add_convert_fusion.2), channel_id=1, source_target_pairs={{0,8},{8,0},{16,24},{24,16},{1,9},{9,1},{17,25},{25,17},{2,10},{10... | collective-permute-start | bytes 184328 | tf_op jit(solution)/shard_map/ppermute | solution.py:555
  23.1 1.0 %shard_map.78 = bf16[64,256]{1,0:T(8,128)(2,1)} custom-call(f32[17,64,128]{2,1,0:T(8,128)S(1)} %get-tuple-element.39.act_second_ref, bf16[128,128]{1,0:T(8,128)(2,1)S(1)} %get-tuple-element.40.pool_second_ref), custom_call_target="tpu_custom_call" | custom-call | tf_op jit(solution)/shard_map/pallas_call | solution.py:646
  24.1 0.6 %collective-permute-done.8 = bf16[240,128]{1,0:T(8,128)(2,1)S(1)} collective-permute-done((bf16[240,128]{1,0:T(8,128)(2,1)S(1)}, bf16[240,128]{1,0:T(8,128)(2,1)S(1)}, u32[]{:S(2)}, u32[]{:S(2)}) %collective-permute-start.8) | collective-permute-done | bytes 61472 | tf_op jit(solution)/shard_map/ppermute | solution.py:555
  24.8 1.5 %collective-permute-done.7 = bf16[240,128]{1,0:T(8,128)(2,1)S(1)} collective-permute-done((bf16[240,128]{1,0:T(8,128)(2,1)S(1)}, bf16[240,128]{1,0:T(8,128)(2,1)S(1)}, u32[]{:S(2)}, u32[]{:S(2)}) %collective-permute-start.7) | collective-permute-done | bytes 61472 | tf_op jit(solution)/shard_map/ppermute | solution.py:555
  26.3 0.5 %collective-permute-done.6 = bf16[240,128]{1,0:T(8,128)(2,1)S(1)} collective-permute-done((bf16[240,128]{1,0:T(8,128)(2,1)S(1)}, bf16[240,128]{1,0:T(8,128)(2,1)S(1)}, u32[]{:S(2)}, u32[]{:S(2)}) %collective-permute-start.6) | collective-permute-done | bytes 61472 | tf_op jit(solution)/shard_map/ppermute | solution.py:555
  26.8 1.3 %collective-permute-start.11 = (bf16[240,128]{1,0:T(8,128)(2,1)S(1)}, bf16[240,128]{1,0:T(8,128)(2,1)S(1)}, u32[]{:S(2)}, u32[]{:S(2)}) collective-permute-start(bf16[240,128]{1,0:T(8,128)(2,1)S(1)} %add_convert_fusion.1), channel_id=1, source_target_pairs={{0,3},{1,2},{2,1},{3,0},{4,7},{5,6},{6,5},{7,4},{8,11},{9,10},{10,... | collective-permute-start | bytes 184328 | tf_op jit(solution)/shard_map/ppermute | solution.py:555
  28.1 1.7 %collective-permute-start.10 = (bf16[240,128]{1,0:T(8,128)(2,1)S(1)}, bf16[240,128]{1,0:T(8,128)(2,1)S(1)}, u32[]{:S(2)}, u32[]{:S(2)}) collective-permute-start(bf16[240,128]{1,0:T(8,128)(2,1)S(1)} %add_convert_fusion.1), channel_id=1, source_target_pairs={{0,2},{1,3},{2,0},{3,1},{4,6},{5,7},{6,4},{7,5},{8,10},{9,11},{10,... | collective-permute-start | bytes 184328 | tf_op jit(solution)/shard_map/ppermute | solution.py:555
  29.8 1.5 %collective-permute-start.9 = (bf16[240,128]{1,0:T(8,128)(2,1)S(1)}, bf16[240,128]{1,0:T(8,128)(2,1)S(1)}, u32[]{:S(2)}, u32[]{:S(2)}) collective-permute-start(bf16[240,128]{1,0:T(8,128)(2,1)S(1)} %add_convert_fusion.1), channel_id=1, source_target_pairs={{0,1},{1,0},{2,3},{3,2},{4,5},{5,4},{6,7},{7,6},{8,9},{9,8},{10,11... | collective-permute-start | bytes 184328 | tf_op jit(solution)/shard_map/ppermute | solution.py:555
  31.3 1.7 %collective-permute-done.11 = bf16[240,128]{1,0:T(8,128)(2,1)S(1)} collective-permute-done((bf16[240,128]{1,0:T(8,128)(2,1)S(1)}, bf16[240,128]{1,0:T(8,128)(2,1)S(1)}, u32[]{:S(2)}, u32[]{:S(2)}) %collective-permute-start.11) | collective-permute-done | bytes 61472 | tf_op jit(solution)/shard_map/ppermute | solution.py:555
  33.0 1.5 %collective-permute-done.10 = bf16[240,128]{1,0:T(8,128)(2,1)S(1)} collective-permute-done((bf16[240,128]{1,0:T(8,128)(2,1)S(1)}, bf16[240,128]{1,0:T(8,128)(2,1)S(1)}, u32[]{:S(2)}, u32[]{:S(2)}) %collective-permute-start.10) | collective-permute-done | bytes 61472 | tf_op jit(solution)/shard_map/ppermute | solution.py:555
  34.7 0.7 %copy.9 = f32[1,32,1,1,2048]{4,3,2,1,0:T(1,128)} copy(f32[1,32,1,1,2048]{4,3,2,1,0:T(1,128)S(1)} %bitcast.17) | data formatting | bytes 524288
  35.4 0.5 %collective-permute-done.12.other_ref = bf16[240,128]{1,0:T(8,128)(2,1)S(1)} collective-permute-done((bf16[240,128]{1,0:T(8,128)(2,1)S(1)}, bf16[240,128]{1,0:T(8,128)(2,1)S(1)}, u32[]{:S(2)}, u32[]{:S(2)}) %collective-permute-start.12) | collective-permute-done | bytes 61472 | tf_op jit(solution)/shard_map/ppermute | solution.py:551
  36.0 0.9 %shard_map.79 = (f32[3,288,64]{2,1,0:T(8,128)}, f32[27,4,32]{2,1,0:T(4,128)}) custom-call(bf16[240,128]{1,0:T(8,128)(2,1)S(1)} %add_convert_fusion.mine_ref, bf16[240,128]{1,0:T(8,128)(2,1)S(1)} %collective-permute-done.12.other_ref), custom_call_target="tpu_custom_call" | custom-call | tf_op jit(solution)/shard_map/pallas_call | solution.py:651
  (13 shorter events, 0.5 us)
Async XLA Ops:
  1.9 8.1 %collective-permute-start = (bf16[48,512]{1,0:T(8,128)(2,1)S(1)}, bf16[48,512]{1,0:T(8,128)(2,1)S(1)}, u32[]{:S(2)}, u32[]{:S(2)}) collective-permute-start(bf16[48,512]{1,0:T(8,128)(2,1)S(1)} %get-tuple-element.26), channel_id=1, source_target_pairs={{0,4},{4,0},{1,5},{5,1},{2,6},{6,2},{3,7},{7,3},{8,12},{12,8},{9,1... | collective-permute-start | bytes 147464 | tf_op jit(solution)/shard_map/ppermute | solution.py:606
  2.4 7.6 %collective-permute-start.1 = (bf16[160,128]{1,0:T(8,128)(2,1)S(1)}, bf16[160,128]{1,0:T(8,128)(2,1)S(1)}, u32[]{:S(2)}, u32[]{:S(2)}) collective-permute-start(bf16[160,128]{1,0:T(8,128)(2,1)S(1)} %get-tuple-element.27), channel_id=1, source_target_pairs={{0,1},{1,0},{2,3},{3,2},{4,5},{5,4},{6,7},{7,6},{8,9},{9,8},{10,11... | collective-permute-start | bytes 122888 | tf_op jit(solution)/shard_map/ppermute | solution.py:604
  5.1 4.9 %collective-permute-start.2 = (bf16[160,128]{1,0:T(8,128)(2,1)S(1)}, bf16[160,128]{1,0:T(8,128)(2,1)S(1)}, u32[]{:S(2)}, u32[]{:S(2)}) collective-permute-start(bf16[160,128]{1,0:T(8,128)(2,1)S(1)} %get-tuple-element.28), channel_id=1, source_target_pairs={{0,4},{1,2},{2,1},{3,7},{4,0},{5,6},{6,5},{7,3},{8,12},{9,10},{10,... | collective-permute-start | bytes 122888 | tf_op jit(solution)/shard_map/ppermute | solution.py:596
  5.2 4.7 %collective-permute-start.3 = (bf16[48,128]{1,0:T(8,128)(2,1)S(1)}, bf16[48,128]{1,0:T(8,128)(2,1)S(1)}, u32[]{:S(2)}, u32[]{:S(2)}) collective-permute-start(bf16[48,128]{1,0:T(8,128)(2,1)S(1)} %get-tuple-element.29), channel_id=1, source_target_pairs={{0,5},{1,4},{2,7},{3,6},{4,1},{5,0},{6,3},{7,2},{8,13},{9,12},{10,... | collective-permute-start | bytes 36872 | tf_op jit(solution)/shard_map/ppermute | solution.py:596
  7.7 2.3 %collective-permute-start.4 = (bf16[48,128]{1,0:T(8,128)(2,1)S(1)}, bf16[48,128]{1,0:T(8,128)(2,1)S(1)}, u32[]{:S(2)}, u32[]{:S(2)}) collective-permute-start(bf16[48,128]{1,0:T(8,128)(2,1)S(1)} %get-tuple-element.30.after_ref), channel_id=1, source_target_pairs={{0,4},{1,6},{2,5},{3,7},{4,0},{5,2},{6,1},{7,3},{8,12},{9,14},{10,... | collective-permute-start | bytes 36872 | tf_op jit(solution)/shard_map/ppermute | solution.py:596
  8.3 1.7 %copy-start = (bf16[1,64,1,1,256]{4,1,3,2,0:T(8,128)(2,1)S(1)}, bf16[1,64,1,1,256]{4,1,3,2,0:T(8,128)(2,1)}, u32[]{:S(2)}) copy-start(bf16[1,64,1,1,256]{4,1,3,2,0:T(8,128)(2,1)} %param.7) | copy-start | bytes 98308
  18.2 1.3 %collective-permute-start.5 = (bf16[240,128]{1,0:T(8,128)(2,1)S(1)}, bf16[240,128]{1,0:T(8,128)(2,1)S(1)}, u32[]{:S(2)}, u32[]{:S(2)}) collective-permute-start(bf16[240,128]{1,0:T(8,128)(2,1)S(1)} %get-tuple-element.38), channel_id=1, source_target_pairs={{0,4},{4,0},{1,5},{5,1},{2,6},{6,2},{3,7},{7,3},{8,12},{12,8},{9,1... | collective-permute-start | bytes 184328 | tf_op jit(solution)/shard_map/ppermute | solution.py:551
  19.5 5.2 %collective-permute-start.8 = (bf16[240,128]{1,0:T(8,128)(2,1)S(1)}, bf16[240,128]{1,0:T(8,128)(2,1)S(1)}, u32[]{:S(2)}, u32[]{:S(2)}) collective-permute-start(bf16[240,128]{1,0:T(8,128)(2,1)S(1)} %add_convert_fusion.2), channel_id=1, source_target_pairs={{0,24},{8,16},{16,8},{24,0},{1,25},{9,17},{17,9},{25,1},{2,26},{10... | collective-permute-start | bytes 184328 | tf_op jit(solution)/shard_map/ppermute | solution.py:555
  22.1 4.2 %collective-permute-start.7 = (bf16[240,128]{1,0:T(8,128)(2,1)S(1)}, bf16[240,128]{1,0:T(8,128)(2,1)S(1)}, u32[]{:S(2)}, u32[]{:S(2)}) collective-permute-start(bf16[240,128]{1,0:T(8,128)(2,1)S(1)} %add_convert_fusion.2), channel_id=1, source_target_pairs={{0,16},{8,24},{16,0},{24,8},{1,17},{9,25},{17,1},{25,9},{2,18},{10... | collective-permute-start | bytes 184328 | tf_op jit(solution)/shard_map/ppermute | solution.py:555
  22.6 4.2 %collective-permute-start.6 = (bf16[240,128]{1,0:T(8,128)(2,1)S(1)}, bf16[240,128]{1,0:T(8,128)(2,1)S(1)}, u32[]{:S(2)}, u32[]{:S(2)}) collective-permute-start(bf16[240,128]{1,0:T(8,128)(2,1)S(1)} %add_convert_fusion.2), channel_id=1, source_target_pairs={{0,8},{8,0},{16,24},{24,16},{1,9},{9,1},{17,25},{25,17},{2,10},{10... | collective-permute-start | bytes 184328 | tf_op jit(solution)/shard_map/ppermute | solution.py:555
  26.8 6.2 %collective-permute-start.11 = (bf16[240,128]{1,0:T(8,128)(2,1)S(1)}, bf16[240,128]{1,0:T(8,128)(2,1)S(1)}, u32[]{:S(2)}, u32[]{:S(2)}) collective-permute-start(bf16[240,128]{1,0:T(8,128)(2,1)S(1)} %add_convert_fusion.1), channel_id=1, source_target_pairs={{0,3},{1,2},{2,1},{3,0},{4,7},{5,6},{6,5},{7,4},{8,11},{9,10},{10,... | collective-permute-start | bytes 184328 | tf_op jit(solution)/shard_map/ppermute | solution.py:555
  28.1 6.4 %collective-permute-start.10 = (bf16[240,128]{1,0:T(8,128)(2,1)S(1)}, bf16[240,128]{1,0:T(8,128)(2,1)S(1)}, u32[]{:S(2)}, u32[]{:S(2)}) collective-permute-start(bf16[240,128]{1,0:T(8,128)(2,1)S(1)} %add_convert_fusion.1), channel_id=1, source_target_pairs={{0,2},{1,3},{2,0},{3,1},{4,6},{5,7},{6,4},{7,5},{8,10},{9,11},{10,... | collective-permute-start | bytes 184328 | tf_op jit(solution)/shard_map/ppermute | solution.py:555
  29.8 4.8 %collective-permute-start.9 = (bf16[240,128]{1,0:T(8,128)(2,1)S(1)}, bf16[240,128]{1,0:T(8,128)(2,1)S(1)}, u32[]{:S(2)}, u32[]{:S(2)}) collective-permute-start(bf16[240,128]{1,0:T(8,128)(2,1)S(1)} %add_convert_fusion.1), channel_id=1, source_target_pairs={{0,1},{1,0},{2,3},{3,2},{4,5},{5,4},{6,7},{7,6},{8,9},{9,8},{10,11... | collective-permute-start | bytes 184328 | tf_op jit(solution)/shard_map/ppermute | solution.py:555
  34.6 1.3 %collective-permute-start.12 = (bf16[240,128]{1,0:T(8,128)(2,1)S(1)}, bf16[240,128]{1,0:T(8,128)(2,1)S(1)}, u32[]{:S(2)}, u32[]{:S(2)}) collective-permute-start(bf16[240,128]{1,0:T(8,128)(2,1)S(1)} %add_convert_fusion.mine_ref), channel_id=1, source_target_pairs={{0,4},{4,0},{1,5},{5,1},{2,6},{6,2},{3,7},{7,3},{8,12},{12,8},{9,1... | collective-permute-start | bytes 184328 | tf_op jit(solution)/shard_map/ppermute | solution.py:551
where the time goes:
time: 37 us; the launch traced here: 36.8 us
  starting transfers between devices  14.7 us (40%)
  Pallas kernels  12.9 us (35%)
  waiting for transfers between devices  7.68 us (21%)
  between operations  0.73 us (2%)
  local copies, waits for them, and re-layouts  0.71 us (2%)
    pallas_call x1, Pallas kernels, on_device_kernels(): call(functools.partial(main_kernel, rows_y), [((NS, 64, MID), F32), ((32,...  8.18 us
    ppermute x6, starting transfers between devices, sum_of_four(): lax.ppermute(part, axis, [(i, i ^ k) for i in range(4)])  8.01 us
    ppermute x6, waiting for transfers between devices, sum_of_four(): lax.ppermute(part, axis, [(i, i ^ k) for i in range(4)])  5.98 us
    ppermute x3, starting transfers between devices, paired(): return lax.ppermute(values, ('gx', 'yz'), routes)  3.27 us
    ppermute x1, starting transfers between devices, on_device_kernels(): got_near = lax.ppermute(near, 'yz', [(i, i ^ 1) for i in range(rows_y)])  2.65 us
    ppermute x2, waiting for transfers between devices, swap_cores(): return lax.ppermute(values, 'gx', [(0, 1), (1, 0)])  1.68 us
    pallas_call x1, Pallas kernels, on_device_kernels(): call(prepare_kernel, [((64, 144), BF16), ((256, 1728), BF16), ((128, 3456...  1.61 us
    pallas_call x1, Pallas kernels, on_device_kernels(): call(pack_kernel, [((136, OWN), F32), ((48, OWN), BF16), ((160, 128), BF1...  1.26 us
  transfers between devices with their start and end apart: 13, of which 8 were waited for; matrix products, arithmetic and copies ran while one was open for 2% of the time, Pallas kernels for 7%

commit v1 on v0

--- a/solution.py
+++ b/solution.py
@@ -182,7 +182,7 @@
     return lax.dot_general(a, b, (((1,), (1,)), ((), ())), preferred_element_type=F32)
 
 
-def pack_kernel(vol_ref, cot_ref, own_ref, x_ref, near_ref, far_ref, xnear_ref, xfar_ref):
+def pack_kernel(vol_ref, cot_ref, own_ref, x_ref, near_ref, far_ref):
     gx = lax.axis_index("gx")
     odd = lax.axis_index("yz") % 2
     own_ref[0:8, :] = jnp.zeros((8, OWN), F32)
@@ -200,17 +200,13 @@
     x_ref[32:48, 0:128] = fold_rows(end).astype(BF16)
     x_ref[32:48, 128:OWN] = jnp.zeros((16, OWN - 128), BF16)
     rims = dot(cot, rim_table())
-    for low, side_ref, xside_ref in ((odd, near_ref, xnear_ref), (1 - odd, far_ref, xfar_ref)):
+    for low, side_ref in ((odd, near_ref), (1 - odd, far_ref)):
         lanes = pl.ds(pl.multiple_of((OWN - 128) * (1 - low), 128), 128)
         tail = jnp.concatenate([own_ref[128:136, lanes], blank[:, 0:128]])
         side_ref[0:128, :] = own_ref[0:128, lanes].astype(BF16)
         side_ref[128:144, :] = tail.astype(BF16)
-        edge = jnp.concatenate([own_ref[pl.ds(start, 24), lanes], blank[:, 0:128]])
-        xside_ref[0:32, :] = edge.astype(BF16)
         rim = jnp.where(low == 1, rims[:, 0:128], rims[:, 128:256])
         side_ref[144:160, :] = fold_rows(rim).astype(BF16)
-        corner = jnp.where(first, pltpu.roll(rim, 100, 1), rim)
-        xside_ref[32:48, :] = fold_rows(corner).astype(BF16)
 
 
 def prepare_kernel(
@@ -289,8 +285,6 @@
     rx_ref,
     rnear_ref,
     rfar_ref,
-    rxnear_ref,
-    rxfar_ref,
     w1_ref,
     w2_ref,
     w3_ref,
@@ -330,8 +324,8 @@
     vol[pl.ds(2 * gx, 17), :, OWN + 128 : FINE] = down[0:136].reshape(17, 8, 128)
     vol[pl.ds(2 * gx, 17), :, 0:OWN] = own_ref[...]
     end = pl.ds(16 * (1 - gx), 3)
-    vol[end, :, 0:OWN] += rx_ref[0:32, :].astype(F32)[0:24].reshape(3, 8, OWN)
-    up, down = above_below(rxnear_ref[0:32, :], rxfar_ref[0:32, :])
+    vol[end, :, 0:OWN] += rx_ref[0:32, 0:OWN].astype(F32)[0:24].reshape(3, 8, OWN)
+    up, down = above_below(rx_ref[0:32, OWN : OWN + 128], rx_ref[0:32, OWN + 128 : FINE])
     vol[end, :, OWN : OWN + 128] += up[0:24].reshape(3, 8, 128)
     vol[end, :, OWN + 128 : FINE] += down[0:24].reshape(3, 8, 128)
 
@@ -355,12 +349,13 @@
         )
         for p in range(8)
     ]
-    up, down = above_below(rxnear_ref[32:48, :], rxfar_ref[32:48, :])
+    up, down = above_below(rx_ref[32:48, OWN : OWN + 128], rx_ref[32:48, OWN + 128 : FINE])
+    up, down = unfold_rows(up), unfold_rows(down)
     planes.append(
         upstream(
             unfold_rows(rx_ref[32:48, 0:128].astype(F32)),
-            moved_to(unfold_rows(up), 0, 32),
-            moved_to(unfold_rows(down), 0, 36),
+            jnp.where(gx == 0, moved_to(up, 0, 32), moved_to(up, 28, 32)),
+            jnp.where(gx == 0, moved_to(down, 0, 36), moved_to(down, 28, 36)),
         )
     )
     spread = dot(jnp.concatenate(planes, axis=0), spread_second_ref[...])
@@ -371,18 +366,22 @@
     lane_fine = lax.broadcasted_iota(jnp.int32, (16, FINE), 1)
     near = lax.broadcasted_iota(jnp.int32, (16, 128), 1) < 64
 
-    def first_layer(j):
-        tile = jnp.concatenate([vol[j], vol[j + 1]], axis=0).astype(BF16)
-        parts = []
-        for moved in shifted(tile, CZ, lane_fine):
-            edge = jnp.where(near, moved[:, OWN : OWN + 128], moved[:, OWN + 128 : FINE])
-            parts.append(jnp.concatenate([moved[:, 0:OWN], edge], axis=1))
-        cols = jnp.concatenate(parts, axis=0)
-        cols_first[j] = cols[:, 0:OWN]
-        pre = dot(w1_ref[...], cols)
-        pre_first[j] = pre[:, 0:OWN]
-        sloped = leaky(pre)
-        pooled_first[j] = pooled(sloped[0:32] + sloped[32:64], CZ)
+    def two_first(first):
+        both = []
+        for j in (first, first + 1):
+            tile = jnp.concatenate([vol[j], vol[j + 1]], axis=0).astype(BF16)
+            parts = []
+            for moved in shifted(tile, CZ, lane_fine):
+                edge = jnp.where(near, moved[:, OWN : OWN + 128], moved[:, OWN + 128 : FINE])
+                parts.append(jnp.concatenate([moved[:, 0:OWN], edge], axis=1))
+            both.append(jnp.concatenate(parts, axis=0))
+            cols_first[j] = both[-1][:, 0:OWN]
+        wide = dot(w1_ref[...], jnp.concatenate(both, axis=1))
+        for k in range(2):
+            pre = wide[:, KEPT * k : KEPT * k + KEPT]
+            pre_first[first + k] = pre[:, 0:OWN]
+            sloped = leaky(pre)
+            pooled_first[first + k] = pooled(sloped[0:32] + sloped[32:64], CZ)
 
     lane = lax.broadcasted_iota(jnp.int32, (32, COARSE), 1)
     valid = jnp.logical_or(
@@ -393,13 +392,13 @@
         ),
     )
 
-    def columns_second(step):
-        six = pooled_first[6 * step : 6 * step + 6].reshape(192, KEPT)
-        picked = dot(six, pool_first_ref[...])
-        for k in range(6):
+    def columns_second(start, count):
+        planes = pooled_first[start : start + count].reshape(32 * count, KEPT)
+        picked = dot(planes, pool_first_ref[...])
+        for k in range(count):
             plane = jnp.where(valid, picked[k * 32 : k * 32 + 32], 0.0).astype(BF16)
             parts = shifted(plane, CZ // 2, lane)
-            cols_second[6 * step + k + 1] = jnp.concatenate(parts, axis=0)
+            cols_second[start + k + 1] = jnp.concatenate(parts, axis=0)
 
     lane_grad = lax.broadcasted_iota(jnp.int32, (64, COARSE), 1)
 
@@ -457,11 +456,13 @@
     for k in (0, 1, 18, 19):
         grad_own[k] = jnp.zeros((64, MID), BF16)
 
-    for step in range(3):
-        for j in range(6 * step, 6 * step + 6):
-            first_layer(j)
-        columns_second(step)
-        four_second(4 * step)
+    for start, count in ((0, 10), (10, 8)):
+        for j in range(start, start + count, 2):
+            two_first(j)
+        columns_second(start, count)
+        four_second(start // 10 * 8)
+        if not start:
+            four_second(4)
     eight_back(0)
     four_second(12)
     last = cols_second[pl.ds(NS - 1 + gx, 3)].reshape(864, COARSE)
@@ -561,15 +562,13 @@
     cot = cotangent.reshape(64, 256)
     k1 = first_kernel.transpose(2, 3, 4, 1, 0).reshape(27, 4, 32)
     k2 = second_kernel.transpose(2, 3, 4, 1, 0).reshape(864, 64)
-    own, x_face, near, far, x_near, x_far = call(
+    own, x_face, near, far = call(
         pack_kernel,
         [
             ((136, OWN), F32),
             ((48, OWN), BF16),
             ((160, 128), BF16),
             ((160, 128), BF16),
-            ((48, 128), BF16),
-            ((48, 128), BF16),
         ],
         16,
     )(in_hbm(volumes.reshape(4, CX * OWN)), in_hbm(cot))
@@ -587,25 +586,22 @@
         16,
         [((144, 64), F32)],
         pl.CostEstimate(flops=10**8, bytes_accessed=2 * 10**6, transcendentals=0),
-    )(x_far, in_hbm(k1), in_hbm(k2))
-
-    def paired(values, partner):
-        routes = [
-            (g * rows_y + i, partner(g, i)) for g in range(2) for i in range(rows_y)
-        ]
-        return lax.ppermute(values, ("gx", "yz"), routes)
-
-    def other_side(g, i, across):
+    )(far, in_hbm(k1), in_hbm(k2))
+
+    def other_side(g, i):
         j = i + (1 if i % 2 else -1)
-        if 0 <= j < rows_y:
-            return (g ^ across) * rows_y + j
-        return (1 - g) * rows_y + i
-
+        return g * rows_y + j if 0 <= j < rows_y else (1 - g) * rows_y + i
+
+    routes = [(g * rows_y + i, other_side(g, i)) for g in range(2) for i in range(rows_y)]
     got_near = lax.ppermute(near, "yz", [(i, i ^ 1) for i in range(rows_y)])
-    got_far = paired(far, lambda g, i: other_side(g, i, 0))
-    got_x = lax.ppermute(x_face, "gx", [(0, 1), (1, 0)])
-    got_x_near = paired(x_near, lambda g, i: (1 - g) * rows_y + (i ^ 1))
-    got_x_far = paired(x_far, lambda g, i: other_side(g, i, 1))
+    got_far = lax.ppermute(far, ("gx", "yz"), routes)
+    x_face, spread_first = lax.optimization_barrier((x_face, spread_first))
+    start = 112 * (1 - lax.axis_index("gx"))
+    strips = [
+        jnp.concatenate([lax.dynamic_slice(got, (start, 0), (32, 128)), got[144:160]])
+        for got in (got_near, got_far)
+    ]
+    got_x = swap_cores(jnp.concatenate([x_face] + strips, axis=1))
 
     act_second, act_grad, kept, sent = call(
         functools.partial(main_kernel, rows_y),
@@ -636,8 +632,6 @@
         got_x,
         got_near,
         got_far,
-        got_x_near,
-        got_x_far,
         *weights,
         pool_first,
         spread_first,

time: 37 us -> 37.9 us (1.024)
  waiting for transfers between devices: 7.68 us -> 10.7 us
  starting transfers between devices: 14.7 us -> 12.1 us
  Pallas kernels: 12.9 us -> 13.4 us
    ppermute x4 -> x1, starting transfers between devices: 3.78 us -> 0.01 us  [on_device_kernels(): got_far = lax.ppermute(far, ('gx', 'yz'), routes)]
    ppermute x6, waiting for transfers between devices: 5.98 us -> 7.76 us  [sum_of_four(): lax.ppermute(part, axis, [(i, i ^ k) for i in range(4)])]
    ppermute x2 -> x3, waiting for transfers between devices: 1.68 us -> 2.55 us  [swap_cores(): return lax.ppermute(values, 'gx', [(0, 1), (1, 0)])]
    pallas_call x1, Pallas kernels: 8.18 us -> 8.75 us  [on_device_kernels(): call(functools.partial(main_kernel, rows_y), [((NS, 64, MID), F32), ((32,...]
    ppermute x2 -> x3, starting transfers between devices: 0.23 us -> 0.69 us  [swap_cores(): return lax.ppermute(values, 'gx', [(0, 1), (1, 0)])]
    ppermute x1, starting transfers between devices: 2.65 us -> 3.09 us  [on_device_kernels(): got_near = lax.ppermute(near, 'yz', [(i, i ^ 1) for i in range(rows_y)])]
  transfers between devices with their start and end apart: 13 -> 11, of which waited for: 8 -> 9; matrix products, arithmetic and copies ran while one was open for 2% -> 2% of each run, Pallas kernels for 7% -> 7%
where the time goes in v1:
time: 37.9 us; the launch traced here: 37.8 us
  Pallas kernels  13.4 us (35%)
  starting transfers between devices  12.1 us (32%)
  waiting for transfers between devices  10.7 us (28%)
  local copies, waits for them, and re-layouts  0.73 us (2%)
  between operations  0.71 us (2%)
    pallas_call x1, Pallas kernels, on_device_kernels(): call(functools.partial(main_kernel, rows_y), [((NS, 64, MID), F32), ((32,...  8.75 us
    ppermute x6, starting transfers between devices, sum_of_four(): lax.ppermute(part, axis, [(i, i ^ k) for i in range(4)])  8.35 us
    ppermute x6, waiting for transfers between devices, sum_of_four(): lax.ppermute(part, axis, [(i, i ^ k) for i in range(4)])  7.76 us
    ppermute x1, starting transfers between devices, on_device_kernels(): got_near = lax.ppermute(near, 'yz', [(i, i ^ 1) for i in range(rows_y)])  3.09 us
    ppermute x3, waiting for transfers between devices, swap_cores(): return lax.ppermute(values, 'gx', [(0, 1), (1, 0)])  2.55 us
    pallas_call x1, Pallas kernels, on_device_kernels(): call(prepare_kernel, [((64, 144), BF16), ((256, 1728), BF16), ((128, 3456...  1.61 us
    pallas_call x1, Pallas kernels, on_device_kernels(): call(pack_kernel, [((136, OWN), F32), ((48, OWN), BF16), ((160, 128), BF1...  1.16 us
    pallas_call x1, Pallas kernels, on_device_kernels(): call(features_kernel, [((64, 256), BF16)], 8)(act_second, pool_second)  1.02 us
  transfers between devices with their start and end apart: 11, of which 9 were waited for; matrix products, arithmetic and copies ran while one was open for 2% of the time, Pallas kernels for 7%

profile of v1, /device:TPU:0, one launch (start us, length us, event | category | flops | bytes accessed | tf_op | source)
XLA Modules:
  0.0 37.8 jit_solution(14511732675079653069)
XLA Ops:
  0.6 1.2 %shard_map.75 = (f32[136,512]{1,0:T(8,128)S(1)}, bf16[48,512]{1,0:T(8,128)(2,1)S(1)}, bf16[160,128]{1,0:T(8,128)(2,1)S(1)}, bf16[160,128]{1,0:T(8,128)(2,1)S(1)}) custom-call(bf16[4,16384]{1,0:T(4,128)(2,1)} %bitcast.21, bf16[64,256]{1,0:T(8,128)(2,1)} %bitcast.19), custom_call_target="tpu_custom_call" | custom-call | tf_op jit(solution)/shard_map/pallas_call | solution.py:565
  1.8 3.1 %collective-permute-start = (bf16[160,128]{1,0:T(8,128)(2,1)S(1)}, bf16[160,128]{1,0:T(8,128)(2,1)S(1)}, u32[]{:S(2)}, u32[]{:S(2)}) collective-permute-start(bf16[160,128]{1,0:T(8,128)(2,1)S(1)} %get-tuple-element.30), channel_id=1, source_target_pairs={{0,1},{1,0},{2,3},{3,2},{4,5},{5,4},{6,7},{7,6},{8,9},{9,8},{10,11... | collective-permute-start | bytes 122888 | tf_op jit(solution)/shard_map/ppermute | solution.py:596
  4.9 1.6 %shard_map.76 = (bf16[64,144]{1,0:T(8,128)(2,1)S(1)}, bf16[256,1728]{1,0:T(8,128)(2,1)S(1)}, bf16[128,3456]{1,0:T(8,128)(2,1)S(1)}, bf16[640,256]{1,0:T(8,128)(2...) custom-call(bf16[160,128]{1,0:T(8,128)(2,1)S(1)} %get-tuple-element.27.after_ref, ...), custom_call_target="tpu_custom_call" | custom-call | flops 100000000 | bytes 2000000 | tf_op jit(solution)/shard_map/pallas_call | solution.py:575
  6.5 0.4 collective-permute-done.rnear_ref
  6.9 0.3 collective-permute-start.2
  7.2 1.1 %collective-permute-done.2.rx_ref = bf16[48,768]{1,0:T(8,128)(2,1)S(1)} collective-permute-done((bf16[48,768]{1,0:T(8,128)(2,1)S(1)}, bf16[48,768]{1,0:T(8,128)(2,1)S(1)}, u32[]{:S(2)}, u32[]{:S(2)}) %collective-permute-start.2) | collective-permute-done | bytes 73760 | tf_op jit(solution)/shard_map/ppermute | solution.py:552
  8.3 8.8 %shard_map.77 = (f32[17,64,128]{2,1,0:T(8,128)S(1)}, f32[32,16,128]{2,1,0:T(8,128)S(1)}, f32[240,128]{1,0:T(8,128)S(1)}, bf16[240,128]{1,0:T(8,128)(2,1)S(1)}) custom-call(f32[17,8,512]{2,1,0:T(8,128)S(1)} %bitcast.18, bf16[64,256]{1,0:T(8,128)(2,1)S(1)} %bitcast.20, bf16[48,768]{1,0:T(8,128)(2,1)S(1)} %collective-permute-done.2.rx_ref, ...), custom_call_target="tpu_custom_call" | custom-call | tf_op jit(solution)/shard_map/pallas_call | solution.py:606
  17.0 0.4 collective-permute-start.3
  17.4 0.9 %collective-permute-done.3 = bf16[240,128]{1,0:T(8,128)(2,1)S(1)} collective-permute-done((bf16[240,128]{1,0:T(8,128)(2,1)S(1)}, bf16[240,128]{1,0:T(8,128)(2,1)S(1)}, u32[]{:S(2)}, u32[]{:S(2)}) %collective-permute-start.3) | collective-permute-done | bytes 61472 | tf_op jit(solution)/shard_map/ppermute | solution.py:552
  18.4 3.0 %collective-permute-start.6 = (bf16[240,128]{1,0:T(8,128)(2,1)S(1)}, bf16[240,128]{1,0:T(8,128)(2,1)S(1)}, u32[]{:S(2)}, u32[]{:S(2)}) collective-permute-start(bf16[240,128]{1,0:T(8,128)(2,1)S(1)} %add_convert_fusion.2), channel_id=1, source_target_pairs={{0,24},{8,16},{16,8},{24,0},{1,25},{9,17},{17,9},{25,1},{2,26},{10... | collective-permute-start | bytes 184328 | tf_op jit(solution)/shard_map/ppermute | solution.py:556
  21.3 0.5 %collective-permute-start.5 = (bf16[240,128]{1,0:T(8,128)(2,1)S(1)}, bf16[240,128]{1,0:T(8,128)(2,1)S(1)}, u32[]{:S(2)}, u32[]{:S(2)}) collective-permute-start(bf16[240,128]{1,0:T(8,128)(2,1)S(1)} %add_convert_fusion.2), channel_id=1, source_target_pairs={{0,16},{8,24},{16,0},{24,8},{1,17},{9,25},{17,1},{25,9},{2,18},{10... | collective-permute-start | bytes 184328 | tf_op jit(solution)/shard_map/ppermute | solution.py:556
  21.8 0.1 collective-permute-start.4
  22.0 1.0 %shard_map.78 = bf16[64,256]{1,0:T(8,128)(2,1)} custom-call(f32[17,64,128]{2,1,0:T(8,128)S(1)} %get-tuple-element.39.act_second_ref, bf16[128,128]{1,0:T(8,128)(2,1)S(1)} %get-tuple-element.40.pool_second_ref), custom_call_target="tpu_custom_call" | custom-call | tf_op jit(solution)/shard_map/pallas_call | solution.py:640
  23.0 0.8 %collective-permute-done.6 = bf16[240,128]{1,0:T(8,128)(2,1)S(1)} collective-permute-done((bf16[240,128]{1,0:T(8,128)(2,1)S(1)}, bf16[240,128]{1,0:T(8,128)(2,1)S(1)}, u32[]{:S(2)}, u32[]{:S(2)}) %collective-permute-start.6) | collective-permute-done | bytes 61472 | tf_op jit(solution)/shard_map/ppermute | solution.py:556
  23.8 1.8 %collective-permute-done.5 = bf16[240,128]{1,0:T(8,128)(2,1)S(1)} collective-permute-done((bf16[240,128]{1,0:T(8,128)(2,1)S(1)}, bf16[240,128]{1,0:T(8,128)(2,1)S(1)}, u32[]{:S(2)}, u32[]{:S(2)}) %collective-permute-start.5) | collective-permute-done | bytes 61472 | tf_op jit(solution)/shard_map/ppermute | solution.py:556
  25.5 0.5 %collective-permute-done.4 = bf16[240,128]{1,0:T(8,128)(2,1)S(1)} collective-permute-done((bf16[240,128]{1,0:T(8,128)(2,1)S(1)}, bf16[240,128]{1,0:T(8,128)(2,1)S(1)}, u32[]{:S(2)}, u32[]{:S(2)}) %collective-permute-start.4) | collective-permute-done | bytes 61472 | tf_op jit(solution)/shard_map/ppermute | solution.py:556
  26.1 3.7 %collective-permute-start.9 = (bf16[240,128]{1,0:T(8,128)(2,1)S(1)}, bf16[240,128]{1,0:T(8,128)(2,1)S(1)}, u32[]{:S(2)}, u32[]{:S(2)}) collective-permute-start(bf16[240,128]{1,0:T(8,128)(2,1)S(1)} %add_convert_fusion.1), channel_id=1, source_target_pairs={{0,3},{1,2},{2,1},{3,0},{4,7},{5,6},{6,5},{7,4},{8,11},{9,10},{10,... | collective-permute-start | bytes 184328 | tf_op jit(solution)/shard_map/ppermute | solution.py:556
  29.8 0.6 %collective-permute-start.8 = (bf16[240,128]{1,0:T(8,128)(2,1)S(1)}, bf16[240,128]{1,0:T(8,128)(2,1)S(1)}, u32[]{:S(2)}, u32[]{:S(2)}) collective-permute-start(bf16[240,128]{1,0:T(8,128)(2,1)S(1)} %add_convert_fusion.1), channel_id=1, source_target_pairs={{0,2},{1,3},{2,0},{3,1},{4,6},{5,7},{6,4},{7,5},{8,10},{9,11},{10,... | collective-permute-start | bytes 184328 | tf_op jit(solution)/shard_map/ppermute | solution.py:556
  30.4 0.5 %collective-permute-start.7 = (bf16[240,128]{1,0:T(8,128)(2,1)S(1)}, bf16[240,128]{1,0:T(8,128)(2,1)S(1)}, u32[]{:S(2)}, u32[]{:S(2)}) collective-permute-start(bf16[240,128]{1,0:T(8,128)(2,1)S(1)} %add_convert_fusion.1), channel_id=1, source_target_pairs={{0,1},{1,0},{2,3},{3,2},{4,5},{5,4},{6,7},{7,6},{8,9},{9,8},{10,11... | collective-permute-start | bytes 184328 | tf_op jit(solution)/shard_map/ppermute | solution.py:556
  30.9 1.6 %collective-permute-done.9 = bf16[240,128]{1,0:T(8,128)(2,1)S(1)} collective-permute-done((bf16[240,128]{1,0:T(8,128)(2,1)S(1)}, bf16[240,128]{1,0:T(8,128)(2,1)S(1)}, u32[]{:S(2)}, u32[]{:S(2)}) %collective-permute-start.9) | collective-permute-done | bytes 61472 | tf_op jit(solution)/shard_map/ppermute | solution.py:556
  32.5 3.1 %collective-permute-done.8 = bf16[240,128]{1,0:T(8,128)(2,1)S(1)} collective-permute-done((bf16[240,128]{1,0:T(8,128)(2,1)S(1)}, bf16[240,128]{1,0:T(8,128)(2,1)S(1)}, u32[]{:S(2)}, u32[]{:S(2)}) %collective-permute-start.8) | collective-permute-done | bytes 61472 | tf_op jit(solution)/shard_map/ppermute | solution.py:556
  35.7 0.7 %copy.9 = f32[1,32,1,1,2048]{4,3,2,1,0:T(1,128)} copy(f32[1,32,1,1,2048]{4,3,2,1,0:T(1,128)S(1)} %bitcast.17) | data formatting | bytes 524288
  36.4 0.5 %collective-permute-done.10.other_ref = bf16[240,128]{1,0:T(8,128)(2,1)S(1)} collective-permute-done((bf16[240,128]{1,0:T(8,128)(2,1)S(1)}, bf16[240,128]{1,0:T(8,128)(2,1)S(1)}, u32[]{:S(2)}, u32[]{:S(2)}) %collective-permute-start.10) | collective-permute-done | bytes 61472 | tf_op jit(solution)/shard_map/ppermute | solution.py:552
  36.9 0.9 %shard_map.79 = (f32[3,288,64]{2,1,0:T(8,128)}, f32[27,4,32]{2,1,0:T(4,128)}) custom-call(bf16[240,128]{1,0:T(8,128)(2,1)S(1)} %add_convert_fusion.mine_ref, bf16[240,128]{1,0:T(8,128)(2,1)S(1)} %collective-permute-done.10.other_ref), custom_call_target="tpu_custom_call" | custom-call | tf_op jit(solution)/shard_map/pallas_call | solution.py:645
  (14 shorter events, 0.2 us)
Async XLA Ops:
  1.8 5.1 %collective-permute-start = (bf16[160,128]{1,0:T(8,128)(2,1)S(1)}, bf16[160,128]{1,0:T(8,128)(2,1)S(1)}, u32[]{:S(2)}, u32[]{:S(2)}) collective-permute-start(bf16[160,128]{1,0:T(8,128)(2,1)S(1)} %get-tuple-element.30), channel_id=1, source_target_pairs={{0,1},{1,0},{2,3},{3,2},{4,5},{5,4},{6,7},{7,6},{8,9},{9,8},{10,11... | collective-permute-start | bytes 122888 | tf_op jit(solution)/shard_map/ppermute | solution.py:596
  4.9 2.0 %collective-permute-start.1 = (bf16[160,128]{1,0:T(8,128)(2,1)S(1)}, bf16[160,128]{1,0:T(8,128)(2,1)S(1)}, u32[]{:S(2)}, u32[]{:S(2)}) collective-permute-start(bf16[160,128]{1,0:T(8,128)(2,1)S(1)} %get-tuple-element.27.after_ref), channel_id=1, source_target_pairs={{0,4},{1,2},{2,1},{3,7},{4,0},{5,6},{6,5},{7,3},{8,12},{9,10},{10,... | collective-permute-start | bytes 122888 | tf_op jit(solution)/shard_map/ppermute | solution.py:597
  6.9 1.4 %copy-start = (bf16[1,64,1,1,256]{4,1,3,2,0:T(8,128)(2,1)S(1)}, bf16[1,64,1,1,256]{4,1,3,2,0:T(8,128)(2,1)}, u32[]{:S(2)}) copy-start(bf16[1,64,1,1,256]{4,1,3,2,0:T(8,128)(2,1)} %param.7) | copy-start | bytes 98308
  6.9 1.3 %collective-permute-start.2 = (bf16[48,768]{1,0:T(8,128)(2,1)S(1)}, bf16[48,768]{1,0:T(8,128)(2,1)S(1)}, u32[]{:S(2)}, u32[]{:S(2)}) collective-permute-start(bf16[48,768]{1,0:T(8,128)(2,1)S(1)} %maximum_maximum_fusion), channel_id=1, source_target_pairs={{0,4},{4,0},{1,5},{5,1},{2,6},{6,2},{3,7},{7,3},{8,12},{12,8},{9,1... | collective-permute-start | bytes 221192 | tf_op jit(solution)/shard_map/ppermute | solution.py:552
  17.0 1.3 %collective-permute-start.3 = (bf16[240,128]{1,0:T(8,128)(2,1)S(1)}, bf16[240,128]{1,0:T(8,128)(2,1)S(1)}, u32[]{:S(2)}, u32[]{:S(2)}) collective-permute-start(bf16[240,128]{1,0:T(8,128)(2,1)S(1)} %get-tuple-element.38), channel_id=1, source_target_pairs={{0,4},{4,0},{1,5},{5,1},{2,6},{6,2},{3,7},{7,3},{8,12},{12,8},{9,1... | collective-permute-start | bytes 184328 | tf_op jit(solution)/shard_map/ppermute | solution.py:552
  18.4 5.4 %collective-permute-start.6 = (bf16[240,128]{1,0:T(8,128)(2,1)S(1)}, bf16[240,128]{1,0:T(8,128)(2,1)S(1)}, u32[]{:S(2)}, u32[]{:S(2)}) collective-permute-start(bf16[240,128]{1,0:T(8,128)(2,1)S(1)} %add_convert_fusion.2), channel_id=1, source_target_pairs={{0,24},{8,16},{16,8},{24,0},{1,25},{9,17},{17,9},{25,1},{2,26},{10... | collective-permute-start | bytes 184328 | tf_op jit(solution)/shard_map/ppermute | solution.py:556
  21.3 4.2 %collective-permute-start.5 = (bf16[240,128]{1,0:T(8,128)(2,1)S(1)}, bf16[240,128]{1,0:T(8,128)(2,1)S(1)}, u32[]{:S(2)}, u32[]{:S(2)}) collective-permute-start(bf16[240,128]{1,0:T(8,128)(2,1)S(1)} %add_convert_fusion.2), channel_id=1, source_target_pairs={{0,16},{8,24},{16,0},{24,8},{1,17},{9,25},{17,1},{25,9},{2,18},{10... | collective-permute-start | bytes 184328 | tf_op jit(solution)/shard_map/ppermute | solution.py:556
  21.8 4.2 %collective-permute-start.4 = (bf16[240,128]{1,0:T(8,128)(2,1)S(1)}, bf16[240,128]{1,0:T(8,128)(2,1)S(1)}, u32[]{:S(2)}, u32[]{:S(2)}) collective-permute-start(bf16[240,128]{1,0:T(8,128)(2,1)S(1)} %add_convert_fusion.2), channel_id=1, source_target_pairs={{0,8},{8,0},{16,24},{24,16},{1,9},{9,1},{17,25},{25,17},{2,10},{10... | collective-permute-start | bytes 184328 | tf_op jit(solution)/shard_map/ppermute | solution.py:556
  26.1 6.4 %collective-permute-start.9 = (bf16[240,128]{1,0:T(8,128)(2,1)S(1)}, bf16[240,128]{1,0:T(8,128)(2,1)S(1)}, u32[]{:S(2)}, u32[]{:S(2)}) collective-permute-start(bf16[240,128]{1,0:T(8,128)(2,1)S(1)} %add_convert_fusion.1), channel_id=1, source_target_pairs={{0,3},{1,2},{2,1},{3,0},{4,7},{5,6},{6,5},{7,4},{8,11},{9,10},{10,... | collective-permute-start | bytes 184328 | tf_op jit(solution)/shard_map/ppermute | solution.py:556
  29.8 5.8 %collective-permute-start.8 = (bf16[240,128]{1,0:T(8,128)(2,1)S(1)}, bf16[240,128]{1,0:T(8,128)(2,1)S(1)}, u32[]{:S(2)}, u32[]{:S(2)}) collective-permute-start(bf16[240,128]{1,0:T(8,128)(2,1)S(1)} %add_convert_fusion.1), channel_id=1, source_target_pairs={{0,2},{1,3},{2,0},{3,1},{4,6},{5,7},{6,4},{7,5},{8,10},{9,11},{10,... | collective-permute-start | bytes 184328 | tf_op jit(solution)/shard_map/ppermute | solution.py:556
  30.4 5.2 %collective-permute-start.7 = (bf16[240,128]{1,0:T(8,128)(2,1)S(1)}, bf16[240,128]{1,0:T(8,128)(2,1)S(1)}, u32[]{:S(2)}, u32[]{:S(2)}) collective-permute-start(bf16[240,128]{1,0:T(8,128)(2,1)S(1)} %add_convert_fusion.1), channel_id=1, source_target_pairs={{0,1},{1,0},{2,3},{3,2},{4,5},{5,4},{6,7},{7,6},{8,9},{9,8},{10,11... | collective-permute-start | bytes 184328 | tf_op jit(solution)/shard_map/ppermute | solution.py:556
  35.6 1.3 %collective-permute-start.10 = (bf16[240,128]{1,0:T(8,128)(2,1)S(1)}, bf16[240,128]{1,0:T(8,128)(2,1)S(1)}, u32[]{:S(2)}, u32[]{:S(2)}) collective-permute-start(bf16[240,128]{1,0:T(8,128)(2,1)S(1)} %add_convert_fusion.mine_ref), channel_id=1, source_target_pairs={{0,4},{4,0},{1,5},{5,1},{2,6},{6,2},{3,7},{7,3},{8,12},{12,8},{9,1... | collective-permute-start | bytes 184328 | tf_op jit(solution)/shard_map/ppermute | solution.py:552

commit v2 on v0

--- a/solution.py
+++ b/solution.py
@@ -261,11 +261,9 @@
         tile,
         jnp.where(z == period - 1, blank, pltpu.roll(tile, size - 1, 1)),
     )
-    return [
-        pltpu.roll(moved, shift, 1) if shift else moved
-        for shift in (period, 0, size - period)
-        for moved in along
-    ]
+    for shift in (period, 0, size - period):
+        for moved in along:
+            yield pltpu.roll(moved, shift, 1) if shift else moved
 
 
 def pooled(values, period):
@@ -373,13 +371,11 @@
 
     def first_layer(j):
         tile = jnp.concatenate([vol[j], vol[j + 1]], axis=0).astype(BF16)
-        parts = []
-        for moved in shifted(tile, CZ, lane_fine):
+        for n, moved in enumerate(shifted(tile, CZ, lane_fine)):
             edge = jnp.where(near, moved[:, OWN : OWN + 128], moved[:, OWN + 128 : FINE])
-            parts.append(jnp.concatenate([moved[:, 0:OWN], edge], axis=1))
-        cols = jnp.concatenate(parts, axis=0)
-        cols_first[j] = cols[:, 0:OWN]
-        pre = dot(w1_ref[...], cols)
+            cols_first[j, 16 * n : 16 * n + 16, 0:OWN] = moved[:, 0:OWN]
+            cols_first[j, 16 * n : 16 * n + 16, OWN:KEPT] = edge
+        pre = dot(w1_ref[...], cols_first[j])
         pre_first[j] = pre[:, 0:OWN]
         sloped = leaky(pre)
         pooled_first[j] = pooled(sloped[0:32] + sloped[32:64], CZ)
@@ -398,8 +394,8 @@
         picked = dot(six, pool_first_ref[...])
         for k in range(6):
             plane = jnp.where(valid, picked[k * 32 : k * 32 + 32], 0.0).astype(BF16)
-            parts = shifted(plane, CZ // 2, lane)
-            cols_second[6 * step + k + 1] = jnp.concatenate(parts, axis=0)
+            for n, moved in enumerate(shifted(plane, CZ // 2, lane)):
+                cols_second[6 * step + k + 1, 32 * n : 32 * n + 32, :] = moved
 
     lane_grad = lax.broadcasted_iota(jnp.int32, (64, COARSE), 1)
 
@@ -407,8 +403,8 @@
         act_second[k] = leaky(pre[:, 0:MID])
         given = spread_up[(k + gx) // 2]
         rounded = jnp.where(pre > 0, given, SLOPE * given).astype(BF16)
-        parts = [moved[:, 0:MID] for moved in shifted(rounded, CZ // 2, lane_grad)]
-        cols_grad[k + 1] = jnp.concatenate(parts, axis=0)
+        for n, moved in enumerate(shifted(rounded, CZ // 2, lane_grad)):
+            cols_grad[k + 1, 64 * n : 64 * n + 64, :] = moved[:, 0:MID]
         kept = rounded[:, 0:MID]
         if k == 0:
             kept = jnp.where(gx == 0, kept, jnp.zeros_like(kept))
@@ -447,7 +443,7 @@
             pre = pre_first[4 * step + k + 2 * gx]
             parts = [jnp.where(pre[r : r + 32] > 0, whole, less) for r in (0, 32)]
             backs.append(jnp.concatenate(parts, axis=0).astype(BF16))
-        cols = [cols_first[4 * step + k + 2 * gx] for k in range(4)]
+        cols = [cols_first[4 * step + k + 2 * gx][:, 0:OWN] for k in range(4)]
         return dot_lanes(jnp.concatenate(cols, axis=1), jnp.concatenate(backs, axis=1))
 
     cols_second[0] = jnp.zeros((288, COARSE), BF16)
@@ -618,7 +614,7 @@
         32,
         [
             ((19, 8, FINE), F32),
-            ((NF, 144, OWN), BF16),
+            ((NF, 144, KEPT), BF16),
             ((NF, 64, OWN), F32),
             ((NF, 32, KEPT), BF16),
             ((NF + 2, 288, COARSE), BF16),

time: 37 us -> 37 us (level)
  no operation moved by 1% of the time
where the time goes in v2:
time: 37 us; the launch traced here: 36.8 us
  starting transfers between devices  14.7 us (40%)
  Pallas kernels  12.9 us (35%)
  waiting for transfers between devices  7.68 us (21%)
  between operations  0.73 us (2%)
  local copies, waits for them, and re-layouts  0.71 us (2%)
    pallas_call x1, Pallas kernels, on_device_kernels(): call(functools.partial(main_kernel, rows_y), [((NS, 64, MID), F32), ((32,...  8.18 us
    ppermute x6, starting transfers between devices, sum_of_four(): lax.ppermute(part, axis, [(i, i ^ k) for i in range(4)])  8.01 us
    ppermute x6, waiting for transfers between devices, sum_of_four(): lax.ppermute(part, axis, [(i, i ^ k) for i in range(4)])  5.98 us
    ppermute x3, starting transfers between devices, paired(): return lax.ppermute(values, ('gx', 'yz'), routes)  3.27 us
    ppermute x1, starting transfers between devices, on_device_kernels(): got_near = lax.ppermute(near, 'yz', [(i, i ^ 1) for i in range(rows_y)])  2.65 us
    ppermute x2, waiting for transfers between devices, swap_cores(): return lax.ppermute(values, 'gx', [(0, 1), (1, 0)])  1.69 us
    pallas_call x1, Pallas kernels, on_device_kernels(): call(prepare_kernel, [((64, 144), BF16), ((256, 1728), BF16), ((128, 3456...  1.61 us
    pallas_call x1, Pallas kernels, on_device_kernels(): call(pack_kernel, [((136, OWN), F32), ((48, OWN), BF16), ((160, 128), BF1...  1.26 us
  transfers between devices with their start and end apart: 13, of which 8 were waited for; matrix products, arithmetic and copies ran while one was open for 2% of the time, Pallas kernels for 7%

profile of v2, /device:TPU:0, one launch (start us, length us, event | category | flops | bytes accessed | tf_op | source)
XLA Modules:
  0.0 36.8 jit_solution(16547352071768930997)
XLA Ops:
  0.6 1.3 %shard_map.75 = (f32[136,512]{1,0:T(8,128)S(1)}, bf16[48,512]{1,0:T(8,128)(2,1)S(1)}, bf16[160,128]{1,0:T(8,128)(2,1)S(1)}, bf16[160,128]{1,0:T(8,128)(2,1)S(1)}...) custom-call(bf16[4,16384]{1,0:T(4,128)(2,1)} %bitcast.21, bf16[64,256]{1,0:T(8,128)(2,1)} %bitcast.19), custom_call_target="tpu_custom_call" | custom-call | tf_op jit(solution)/shard_map/pallas_call | solution.py:560
  1.9 0.5 %collective-permute-start = (bf16[48,512]{1,0:T(8,128)(2,1)S(1)}, bf16[48,512]{1,0:T(8,128)(2,1)S(1)}, u32[]{:S(2)}, u32[]{:S(2)}) collective-permute-start(bf16[48,512]{1,0:T(8,128)(2,1)S(1)} %get-tuple-element.26), channel_id=1, source_target_pairs={{0,4},{4,0},{1,5},{5,1},{2,6},{6,2},{3,7},{7,3},{8,12},{12,8},{9,1... | collective-permute-start | bytes 147464 | tf_op jit(solution)/shard_map/ppermute | solution.py:602
  2.4 2.7 %collective-permute-start.1 = (bf16[160,128]{1,0:T(8,128)(2,1)S(1)}, bf16[160,128]{1,0:T(8,128)(2,1)S(1)}, u32[]{:S(2)}, u32[]{:S(2)}) collective-permute-start(bf16[160,128]{1,0:T(8,128)(2,1)S(1)} %get-tuple-element.27), channel_id=1, source_target_pairs={{0,1},{1,0},{2,3},{3,2},{4,5},{5,4},{6,7},{7,6},{8,9},{9,8},{10,11... | collective-permute-start | bytes 122888 | tf_op jit(solution)/shard_map/ppermute | solution.py:600
  5.1 0.2 collective-permute-start.2
  5.2 2.5 %collective-permute-start.3 = (bf16[48,128]{1,0:T(8,128)(2,1)S(1)}, bf16[48,128]{1,0:T(8,128)(2,1)S(1)}, u32[]{:S(2)}, u32[]{:S(2)}) collective-permute-start(bf16[48,128]{1,0:T(8,128)(2,1)S(1)} %get-tuple-element.29), channel_id=1, source_target_pairs={{0,5},{1,4},{2,7},{3,6},{4,1},{5,0},{6,3},{7,2},{8,13},{9,12},{10,... | collective-permute-start | bytes 36872 | tf_op jit(solution)/shard_map/ppermute | solution.py:592
  7.7 0.6 %collective-permute-start.4 = (bf16[48,128]{1,0:T(8,128)(2,1)S(1)}, bf16[48,128]{1,0:T(8,128)(2,1)S(1)}, u32[]{:S(2)}, u32[]{:S(2)}) collective-permute-start(bf16[48,128]{1,0:T(8,128)(2,1)S(1)} %get-tuple-element.30.after_ref), channel_id=1, source_target_pairs={{0,4},{1,6},{2,5},{3,7},{4,0},{5,2},{6,1},{7,3},{8,12},{9,14},{10,... | collective-permute-start | bytes 36872 | tf_op jit(solution)/shard_map/ppermute | solution.py:592
  8.3 1.6 %shard_map.76 = (bf16[64,144]{1,0:T(8,128)(2,1)S(1)}, bf16[256,1728]{1,0:T(8,128)(2,1)S(1)}, bf16[128,3456]{1,0:T(8,128)(2,1)S(1)}, bf16[640,256]{1,0:T(8,128)(2...) custom-call(bf16[48,128]{1,0:T(8,128)(2,1)S(1)} %get-tuple-element.30.after_ref, ...), custom_call_target="tpu_custom_call" | custom-call | flops 100000000 | bytes 2000000 | tf_op jit(solution)/shard_map/pallas_call | solution.py:572
  10.0 8.2 %shard_map.77 = (f32[17,64,128]{2,1,0:T(8,128)S(1)}, f32[32,16,128]{2,1,0:T(8,128)S(1)}, f32[240,128]{1,0:T(8,128)S(1)}, bf16[240,128]{1,0:T(8,128)(2,1)S(1)}) custom-call(f32[17,8,512]{2,1,0:T(8,128)S(1)} %bitcast.18, bf16[64,256]{1,0:T(8,128)(2,1)S(1)} %bitcast.20, bf16[48,512]{1,0:T(8,128)(2,1)S(1)} %collective-permute-done.rx_ref, ...), custom_call_target="tpu_custom_call" | custom-call | tf_op jit(solution)/shard_map/pallas_call | solution.py:606
  18.4 1.2 %collective-permute-done.5 = bf16[240,128]{1,0:T(8,128)(2,1)S(1)} collective-permute-done((bf16[240,128]{1,0:T(8,128)(2,1)S(1)}, bf16[240,128]{1,0:T(8,128)(2,1)S(1)}, u32[]{:S(2)}, u32[]{:S(2)}) %collective-permute-start.5) | collective-permute-done | bytes 61472 | tf_op jit(solution)/shard_map/ppermute | solution.py:547
  19.5 2.5 %collective-permute-start.8 = (bf16[240,128]{1,0:T(8,128)(2,1)S(1)}, bf16[240,128]{1,0:T(8,128)(2,1)S(1)}, u32[]{:S(2)}, u32[]{:S(2)}) collective-permute-start(bf16[240,128]{1,0:T(8,128)(2,1)S(1)} %add_convert_fusion.2), channel_id=1, source_target_pairs={{0,24},{8,16},{16,8},{24,0},{1,25},{9,17},{17,9},{25,1},{2,26},{10... | collective-permute-start | bytes 184328 | tf_op jit(solution)/shard_map/ppermute | solution.py:551
  22.1 0.5 %collective-permute-start.7 = (bf16[240,128]{1,0:T(8,128)(2,1)S(1)}, bf16[240,128]{1,0:T(8,128)(2,1)S(1)}, u32[]{:S(2)}, u32[]{:S(2)}) collective-permute-start(bf16[240,128]{1,0:T(8,128)(2,1)S(1)} %add_convert_fusion.2), channel_id=1, source_target_pairs={{0,16},{8,24},{16,0},{24,8},{1,17},{9,25},{17,1},{25,9},{2,18},{10... | collective-permute-start | bytes 184328 | tf_op jit(solution)/shard_map/ppermute | solution.py:551
  22.6 0.5 %collective-permute-start.6 = (bf16[240,128]{1,0:T(8,128)(2,1)S(1)}, bf16[240,128]{1,0:T(8,128)(2,1)S(1)}, u32[]{:S(2)}, u32[]{:S(2)}) collective-permute-start(bf16[240,128]{1,0:T(8,128)(2,1)S(1)} %add_convert_fusion.2), channel_id=1, source_target_pairs={{0,8},{8,0},{16,24},{24,16},{1,9},{9,1},{17,25},{25,17},{2,10},{10... | collective-permute-start | bytes 184328 | tf_op jit(solution)/shard_map/ppermute | solution.py:551
  23.1 1.0 %shard_map.78 = bf16[64,256]{1,0:T(8,128)(2,1)} custom-call(f32[17,64,128]{2,1,0:T(8,128)S(1)} %get-tuple-element.39.act_second_ref, bf16[128,128]{1,0:T(8,128)(2,1)S(1)} %get-tuple-element.40.pool_second_ref), custom_call_target="tpu_custom_call" | custom-call | tf_op jit(solution)/shard_map/pallas_call | solution.py:642
  24.1 0.6 %collective-permute-done.8 = bf16[240,128]{1,0:T(8,128)(2,1)S(1)} collective-permute-done((bf16[240,128]{1,0:T(8,128)(2,1)S(1)}, bf16[240,128]{1,0:T(8,128)(2,1)S(1)}, u32[]{:S(2)}, u32[]{:S(2)}) %collective-permute-start.8) | collective-permute-done | bytes 61472 | tf_op jit(solution)/shard_map/ppermute | solution.py:551
  24.8 1.5 %collective-permute-done.7 = bf16[240,128]{1,0:T(8,128)(2,1)S(1)} collective-permute-done((bf16[240,128]{1,0:T(8,128)(2,1)S(1)}, bf16[240,128]{1,0:T(8,128)(2,1)S(1)}, u32[]{:S(2)}, u32[]{:S(2)}) %collective-permute-start.7) | collective-permute-done | bytes 61472 | tf_op jit(solution)/shard_map/ppermute | solution.py:551
  26.3 0.5 %collective-permute-done.6 = bf16[240,128]{1,0:T(8,128)(2,1)S(1)} collective-permute-done((bf16[240,128]{1,0:T(8,128)(2,1)S(1)}, bf16[240,128]{1,0:T(8,128)(2,1)S(1)}, u32[]{:S(2)}, u32[]{:S(2)}) %collective-permute-start.6) | collective-permute-done | bytes 61472 | tf_op jit(solution)/shard_map/ppermute | solution.py:551
  26.8 1.3 %collective-permute-start.11 = (bf16[240,128]{1,0:T(8,128)(2,1)S(1)}, bf16[240,128]{1,0:T(8,128)(2,1)S(1)}, u32[]{:S(2)}, u32[]{:S(2)}) collective-permute-start(bf16[240,128]{1,0:T(8,128)(2,1)S(1)} %add_convert_fusion.1), channel_id=1, source_target_pairs={{0,3},{1,2},{2,1},{3,0},{4,7},{5,6},{6,5},{7,4},{8,11},{9,10},{10,... | collective-permute-start | bytes 184328 | tf_op jit(solution)/shard_map/ppermute | solution.py:551
  28.1 1.7 %collective-permute-start.10 = (bf16[240,128]{1,0:T(8,128)(2,1)S(1)}, bf16[240,128]{1,0:T(8,128)(2,1)S(1)}, u32[]{:S(2)}, u32[]{:S(2)}) collective-permute-start(bf16[240,128]{1,0:T(8,128)(2,1)S(1)} %add_convert_fusion.1), channel_id=1, source_target_pairs={{0,2},{1,3},{2,0},{3,1},{4,6},{5,7},{6,4},{7,5},{8,10},{9,11},{10,... | collective-permute-start | bytes 184328 | tf_op jit(solution)/shard_map/ppermute | solution.py:551
  29.8 1.5 %collective-permute-start.9 = (bf16[240,128]{1,0:T(8,128)(2,1)S(1)}, bf16[240,128]{1,0:T(8,128)(2,1)S(1)}, u32[]{:S(2)}, u32[]{:S(2)}) collective-permute-start(bf16[240,128]{1,0:T(8,128)(2,1)S(1)} %add_convert_fusion.1), channel_id=1, source_target_pairs={{0,1},{1,0},{2,3},{3,2},{4,5},{5,4},{6,7},{7,6},{8,9},{9,8},{10,11... | collective-permute-start | bytes 184328 | tf_op jit(solution)/shard_map/ppermute | solution.py:551
  31.3 1.7 %collective-permute-done.11 = bf16[240,128]{1,0:T(8,128)(2,1)S(1)} collective-permute-done((bf16[240,128]{1,0:T(8,128)(2,1)S(1)}, bf16[240,128]{1,0:T(8,128)(2,1)S(1)}, u32[]{:S(2)}, u32[]{:S(2)}) %collective-permute-start.11) | collective-permute-done | bytes 61472 | tf_op jit(solution)/shard_map/ppermute | solution.py:551
  33.0 1.5 %collective-permute-done.10 = bf16[240,128]{1,0:T(8,128)(2,1)S(1)} collective-permute-done((bf16[240,128]{1,0:T(8,128)(2,1)S(1)}, bf16[240,128]{1,0:T(8,128)(2,1)S(1)}, u32[]{:S(2)}, u32[]{:S(2)}) %collective-permute-start.10) | collective-permute-done | bytes 61472 | tf_op jit(solution)/shard_map/ppermute | solution.py:551
  34.7 0.7 %copy.9 = f32[1,32,1,1,2048]{4,3,2,1,0:T(1,128)} copy(f32[1,32,1,1,2048]{4,3,2,1,0:T(1,128)S(1)} %bitcast.17) | data formatting | bytes 524288
  35.4 0.5 %collective-permute-done.12.other_ref = bf16[240,128]{1,0:T(8,128)(2,1)S(1)} collective-permute-done((bf16[240,128]{1,0:T(8,128)(2,1)S(1)}, bf16[240,128]{1,0:T(8,128)(2,1)S(1)}, u32[]{:S(2)}, u32[]{:S(2)}) %collective-permute-start.12) | collective-permute-done | bytes 61472 | tf_op jit(solution)/shard_map/ppermute | solution.py:547
  36.0 0.9 %shard_map.79 = (f32[3,288,64]{2,1,0:T(8,128)}, f32[27,4,32]{2,1,0:T(4,128)}) custom-call(bf16[240,128]{1,0:T(8,128)(2,1)S(1)} %add_convert_fusion.mine_ref, bf16[240,128]{1,0:T(8,128)(2,1)S(1)} %collective-permute-done.12.other_ref), custom_call_target="tpu_custom_call" | custom-call | tf_op jit(solution)/shard_map/pallas_call | solution.py:647
  (13 shorter events, 0.4 us)
Async XLA Ops:
  1.9 8.1 %collective-permute-start = (bf16[48,512]{1,0:T(8,128)(2,1)S(1)}, bf16[48,512]{1,0:T(8,128)(2,1)S(1)}, u32[]{:S(2)}, u32[]{:S(2)}) collective-permute-start(bf16[48,512]{1,0:T(8,128)(2,1)S(1)} %get-tuple-element.26), channel_id=1, source_target_pairs={{0,4},{4,0},{1,5},{5,1},{2,6},{6,2},{3,7},{7,3},{8,12},{12,8},{9,1... | collective-permute-start | bytes 147464 | tf_op jit(solution)/shard_map/ppermute | solution.py:602
  2.4 7.6 %collective-permute-start.1 = (bf16[160,128]{1,0:T(8,128)(2,1)S(1)}, bf16[160,128]{1,0:T(8,128)(2,1)S(1)}, u32[]{:S(2)}, u32[]{:S(2)}) collective-permute-start(bf16[160,128]{1,0:T(8,128)(2,1)S(1)} %get-tuple-element.27), channel_id=1, source_target_pairs={{0,1},{1,0},{2,3},{3,2},{4,5},{5,4},{6,7},{7,6},{8,9},{9,8},{10,11... | collective-permute-start | bytes 122888 | tf_op jit(solution)/shard_map/ppermute | solution.py:600
  5.1 4.9 %collective-permute-start.2 = (bf16[160,128]{1,0:T(8,128)(2,1)S(1)}, bf16[160,128]{1,0:T(8,128)(2,1)S(1)}, u32[]{:S(2)}, u32[]{:S(2)}) collective-permute-start(bf16[160,128]{1,0:T(8,128)(2,1)S(1)} %get-tuple-element.28), channel_id=1, source_target_pairs={{0,4},{1,2},{2,1},{3,7},{4,0},{5,6},{6,5},{7,3},{8,12},{9,10},{10,... | collective-permute-start | bytes 122888 | tf_op jit(solution)/shard_map/ppermute | solution.py:592
  5.2 4.7 %collective-permute-start.3 = (bf16[48,128]{1,0:T(8,128)(2,1)S(1)}, bf16[48,128]{1,0:T(8,128)(2,1)S(1)}, u32[]{:S(2)}, u32[]{:S(2)}) collective-permute-start(bf16[48,128]{1,0:T(8,128)(2,1)S(1)} %get-tuple-element.29), channel_id=1, source_target_pairs={{0,5},{1,4},{2,7},{3,6},{4,1},{5,0},{6,3},{7,2},{8,13},{9,12},{10,... | collective-permute-start | bytes 36872 | tf_op jit(solution)/shard_map/ppermute | solution.py:592
  7.7 2.3 %collective-permute-start.4 = (bf16[48,128]{1,0:T(8,128)(2,1)S(1)}, bf16[48,128]{1,0:T(8,128)(2,1)S(1)}, u32[]{:S(2)}, u32[]{:S(2)}) collective-permute-start(bf16[48,128]{1,0:T(8,128)(2,1)S(1)} %get-tuple-element.30.after_ref), channel_id=1, source_target_pairs={{0,4},{1,6},{2,5},{3,7},{4,0},{5,2},{6,1},{7,3},{8,12},{9,14},{10,... | collective-permute-start | bytes 36872 | tf_op jit(solution)/shard_map/ppermute | solution.py:592
  8.3 1.7 %copy-start = (bf16[1,64,1,1,256]{4,1,3,2,0:T(8,128)(2,1)S(1)}, bf16[1,64,1,1,256]{4,1,3,2,0:T(8,128)(2,1)}, u32[]{:S(2)}) copy-start(bf16[1,64,1,1,256]{4,1,3,2,0:T(8,128)(2,1)} %param.7) | copy-start | bytes 98308
  18.2 1.3 %collective-permute-start.5 = (bf16[240,128]{1,0:T(8,128)(2,1)S(1)}, bf16[240,128]{1,0:T(8,128)(2,1)S(1)}, u32[]{:S(2)}, u32[]{:S(2)}) collective-permute-start(bf16[240,128]{1,0:T(8,128)(2,1)S(1)} %get-tuple-element.38), channel_id=1, source_target_pairs={{0,4},{4,0},{1,5},{5,1},{2,6},{6,2},{3,7},{7,3},{8,12},{12,8},{9,1... | collective-permute-start | bytes 184328 | tf_op jit(solution)/shard_map/ppermute | solution.py:547
  19.5 5.2 %collective-permute-start.8 = (bf16[240,128]{1,0:T(8,128)(2,1)S(1)}, bf16[240,128]{1,0:T(8,128)(2,1)S(1)}, u32[]{:S(2)}, u32[]{:S(2)}) collective-permute-start(bf16[240,128]{1,0:T(8,128)(2,1)S(1)} %add_convert_fusion.2), channel_id=1, source_target_pairs={{0,24},{8,16},{16,8},{24,0},{1,25},{9,17},{17,9},{25,1},{2,26},{10... | collective-permute-start | bytes 184328 | tf_op jit(solution)/shard_map/ppermute | solution.py:551
  22.1 4.2 %collective-permute-start.7 = (bf16[240,128]{1,0:T(8,128)(2,1)S(1)}, bf16[240,128]{1,0:T(8,128)(2,1)S(1)}, u32[]{:S(2)}, u32[]{:S(2)}) collective-permute-start(bf16[240,128]{1,0:T(8,128)(2,1)S(1)} %add_convert_fusion.2), channel_id=1, source_target_pairs={{0,16},{8,24},{16,0},{24,8},{1,17},{9,25},{17,1},{25,9},{2,18},{10... | collective-permute-start | bytes 184328 | tf_op jit(solution)/shard_map/ppermute | solution.py:551
  22.6 4.2 %collective-permute-start.6 = (bf16[240,128]{1,0:T(8,128)(2,1)S(1)}, bf16[240,128]{1,0:T(8,128)(2,1)S(1)}, u32[]{:S(2)}, u32[]{:S(2)}) collective-permute-start(bf16[240,128]{1,0:T(8,128)(2,1)S(1)} %add_convert_fusion.2), channel_id=1, source_target_pairs={{0,8},{8,0},{16,24},{24,16},{1,9},{9,1},{17,25},{25,17},{2,10},{10... | collective-permute-start | bytes 184328 | tf_op jit(solution)/shard_map/ppermute | solution.py:551
  26.8 6.2 %collective-permute-start.11 = (bf16[240,128]{1,0:T(8,128)(2,1)S(1)}, bf16[240,128]{1,0:T(8,128)(2,1)S(1)}, u32[]{:S(2)}, u32[]{:S(2)}) collective-permute-start(bf16[240,128]{1,0:T(8,128)(2,1)S(1)} %add_convert_fusion.1), channel_id=1, source_target_pairs={{0,3},{1,2},{2,1},{3,0},{4,7},{5,6},{6,5},{7,4},{8,11},{9,10},{10,... | collective-permute-start | bytes 184328 | tf_op jit(solution)/shard_map/ppermute | solution.py:551
  28.1 6.4 %collective-permute-start.10 = (bf16[240,128]{1,0:T(8,128)(2,1)S(1)}, bf16[240,128]{1,0:T(8,128)(2,1)S(1)}, u32[]{:S(2)}, u32[]{:S(2)}) collective-permute-start(bf16[240,128]{1,0:T(8,128)(2,1)S(1)} %add_convert_fusion.1), channel_id=1, source_target_pairs={{0,2},{1,3},{2,0},{3,1},{4,6},{5,7},{6,4},{7,5},{8,10},{9,11},{10,... | collective-permute-start | bytes 184328 | tf_op jit(solution)/shard_map/ppermute | solution.py:551
  29.8 4.8 %collective-permute-start.9 = (bf16[240,128]{1,0:T(8,128)(2,1)S(1)}, bf16[240,128]{1,0:T(8,128)(2,1)S(1)}, u32[]{:S(2)}, u32[]{:S(2)}) collective-permute-start(bf16[240,128]{1,0:T(8,128)(2,1)S(1)} %add_convert_fusion.1), channel_id=1, source_target_pairs={{0,1},{1,0},{2,3},{3,2},{4,5},{5,4},{6,7},{7,6},{8,9},{9,8},{10,11... | collective-permute-start | bytes 184328 | tf_op jit(solution)/shard_map/ppermute | solution.py:551
  34.6 1.3 %collective-permute-start.12 = (bf16[240,128]{1,0:T(8,128)(2,1)S(1)}, bf16[240,128]{1,0:T(8,128)(2,1)S(1)}, u32[]{:S(2)}, u32[]{:S(2)}) collective-permute-start(bf16[240,128]{1,0:T(8,128)(2,1)S(1)} %add_convert_fusion.mine_ref), channel_id=1, source_target_pairs={{0,4},{4,0},{1,5},{5,1},{2,6},{6,2},{3,7},{7,3},{8,12},{12,8},{9,1... | collective-permute-start | bytes 184328 | tf_op jit(solution)/shard_map/ppermute | solution.py:547

commit v3 on v2

--- a/solution.py
+++ b/solution.py
@@ -641,9 +641,9 @@
     )
     [features] = call(features_kernel, [((64, 256), BF16)], 8)(act_second, pool_second)
     part = (kept + swap_cores(sent).astype(F32)).astype(BF16)
-    part = sum_of_four(part, "dp")
+    part = sum_of_four(part, "yz")
     part, features = lax.optimization_barrier((part, features))
-    mine = sum_of_four(part, "yz")
+    mine = sum_of_four(part, "dp")
     second, first = call(unpack_kernel, [((3, 288, 64), F32), ((27, 4, 32), F32)], 8)(
         mine, swap_cores(mine)
     )

time: 37 us -> 38.3 us (1.035)
  waiting for transfers between devices: 7.68 us -> 9.01 us
    ppermute x6, waiting for transfers between devices: 5.98 us -> 7.31 us  [sum_of_four(): lax.ppermute(part, axis, [(i, i ^ k) for i in range(4)])]
  transfers between devices with their start and end apart: 13 -> 13, of which waited for: 8 -> 7; matrix products, arithmetic and copies ran while one was open for 2% -> 2% of each run, Pallas kernels for 7% -> 7%
where the time goes in v3:
time: 38.3 us; the launch traced here: 38.2 us
  starting transfers between devices  14.7 us (38%)
  Pallas kernels  12.9 us (34%)
  waiting for transfers between devices  9.01 us (24%)
  between operations  0.73 us (2%)
  local copies, waits for them, and re-layouts  0.71 us (2%)
    pallas_call x1, Pallas kernels, on_device_kernels(): call(functools.partial(main_kernel, rows_y), [((NS, 64, MID), F32), ((32,...  8.18 us
    ppermute x6, starting transfers between devices, sum_of_four(): lax.ppermute(part, axis, [(i, i ^ k) for i in range(4)])  8.01 us
    ppermute x6, waiting for transfers between devices, sum_of_four(): lax.ppermute(part, axis, [(i, i ^ k) for i in range(4)])  7.31 us
    ppermute x3, starting transfers between devices, paired(): return lax.ppermute(values, ('gx', 'yz'), routes)  3.27 us
    ppermute x1, starting transfers between devices, on_device_kernels(): got_near = lax.ppermute(near, 'yz', [(i, i ^ 1) for i in range(rows_y)])  2.65 us
    ppermute x2, waiting for transfers between devices, swap_cores(): return lax.ppermute(values, 'gx', [(0, 1), (1, 0)])  1.69 us
    pallas_call x1, Pallas kernels, on_device_kernels(): call(prepare_kernel, [((64, 144), BF16), ((256, 1728), BF16), ((128, 3456...  1.61 us
    pallas_call x1, Pallas kernels, on_device_kernels(): call(pack_kernel, [((136, OWN), F32), ((48, OWN), BF16), ((160, 128), BF1...  1.26 us
  transfers between devices with their start and end apart: 13, of which 7 were waited for; matrix products, arithmetic and copies ran while one was open for 2% of the time, Pallas kernels for 7%

profile of v3, /device:TPU:0, one launch (start us, length us, event | category | flops | bytes accessed | tf_op | source)
XLA Modules:
  0.0 38.2 jit_solution(695821413307698662)
XLA Ops:
  0.6 1.3 %shard_map.75 = (f32[136,512]{1,0:T(8,128)S(1)}, bf16[48,512]{1,0:T(8,128)(2,1)S(1)}, bf16[160,128]{1,0:T(8,128)(2,1)S(1)}, bf16[160,128]{1,0:T(8,128)(2,1)S(1)}...) custom-call(bf16[4,16384]{1,0:T(4,128)(2,1)} %bitcast.21, bf16[64,256]{1,0:T(8,128)(2,1)} %bitcast.19), custom_call_target="tpu_custom_call" | custom-call | tf_op jit(solution)/shard_map/pallas_call | solution.py:560
  1.9 0.5 %collective-permute-start = (bf16[48,512]{1,0:T(8,128)(2,1)S(1)}, bf16[48,512]{1,0:T(8,128)(2,1)S(1)}, u32[]{:S(2)}, u32[]{:S(2)}) collective-permute-start(bf16[48,512]{1,0:T(8,128)(2,1)S(1)} %get-tuple-element.26), channel_id=1, source_target_pairs={{0,4},{4,0},{1,5},{5,1},{2,6},{6,2},{3,7},{7,3},{8,12},{12,8},{9,1... | collective-permute-start | bytes 147464 | tf_op jit(solution)/shard_map/ppermute | solution.py:602
  2.4 2.7 %collective-permute-start.1 = (bf16[160,128]{1,0:T(8,128)(2,1)S(1)}, bf16[160,128]{1,0:T(8,128)(2,1)S(1)}, u32[]{:S(2)}, u32[]{:S(2)}) collective-permute-start(bf16[160,128]{1,0:T(8,128)(2,1)S(1)} %get-tuple-element.27), channel_id=1, source_target_pairs={{0,1},{1,0},{2,3},{3,2},{4,5},{5,4},{6,7},{7,6},{8,9},{9,8},{10,11... | collective-permute-start | bytes 122888 | tf_op jit(solution)/shard_map/ppermute | solution.py:600
  5.1 0.2 collective-permute-start.2
  5.2 2.5 %collective-permute-start.3 = (bf16[48,128]{1,0:T(8,128)(2,1)S(1)}, bf16[48,128]{1,0:T(8,128)(2,1)S(1)}, u32[]{:S(2)}, u32[]{:S(2)}) collective-permute-start(bf16[48,128]{1,0:T(8,128)(2,1)S(1)} %get-tuple-element.29), channel_id=1, source_target_pairs={{0,5},{1,4},{2,7},{3,6},{4,1},{5,0},{6,3},{7,2},{8,13},{9,12},{10,... | collective-permute-start | bytes 36872 | tf_op jit(solution)/shard_map/ppermute | solution.py:592
  7.7 0.6 %collective-permute-start.4 = (bf16[48,128]{1,0:T(8,128)(2,1)S(1)}, bf16[48,128]{1,0:T(8,128)(2,1)S(1)}, u32[]{:S(2)}, u32[]{:S(2)}) collective-permute-start(bf16[48,128]{1,0:T(8,128)(2,1)S(1)} %get-tuple-element.30.after_ref), channel_id=1, source_target_pairs={{0,4},{1,6},{2,5},{3,7},{4,0},{5,2},{6,1},{7,3},{8,12},{9,14},{10,... | collective-permute-start | bytes 36872 | tf_op jit(solution)/shard_map/ppermute | solution.py:592
  8.3 1.6 %shard_map.76 = (bf16[64,144]{1,0:T(8,128)(2,1)S(1)}, bf16[256,1728]{1,0:T(8,128)(2,1)S(1)}, bf16[128,3456]{1,0:T(8,128)(2,1)S(1)}, bf16[640,256]{1,0:T(8,128)(2...) custom-call(bf16[48,128]{1,0:T(8,128)(2,1)S(1)} %get-tuple-element.30.after_ref, ...), custom_call_target="tpu_custom_call" | custom-call | flops 100000000 | bytes 2000000 | tf_op jit(solution)/shard_map/pallas_call | solution.py:572
  10.0 8.2 %shard_map.77 = (f32[17,64,128]{2,1,0:T(8,128)S(1)}, f32[32,16,128]{2,1,0:T(8,128)S(1)}, f32[240,128]{1,0:T(8,128)S(1)}, bf16[240,128]{1,0:T(8,128)(2,1)S(1)}) custom-call(f32[17,8,512]{2,1,0:T(8,128)S(1)} %bitcast.18, bf16[64,256]{1,0:T(8,128)(2,1)S(1)} %bitcast.20, bf16[48,512]{1,0:T(8,128)(2,1)S(1)} %collective-permute-done.rx_ref, ...), custom_call_target="tpu_custom_call" | custom-call | tf_op jit(solution)/shard_map/pallas_call | solution.py:606
  18.4 1.2 %collective-permute-done.5 = bf16[240,128]{1,0:T(8,128)(2,1)S(1)} collective-permute-done((bf16[240,128]{1,0:T(8,128)(2,1)S(1)}, bf16[240,128]{1,0:T(8,128)(2,1)S(1)}, u32[]{:S(2)}, u32[]{:S(2)}) %collective-permute-start.5) | collective-permute-done | bytes 61472 | tf_op jit(solution)/shard_map/ppermute | solution.py:547
  19.5 1.3 %collective-permute-start.8 = (bf16[240,128]{1,0:T(8,128)(2,1)S(1)}, bf16[240,128]{1,0:T(8,128)(2,1)S(1)}, u32[]{:S(2)}, u32[]{:S(2)}) collective-permute-start(bf16[240,128]{1,0:T(8,128)(2,1)S(1)} %add_convert_fusion.2), channel_id=1, source_target_pairs={{0,3},{1,2},{2,1},{3,0},{4,7},{5,6},{6,5},{7,4},{8,11},{9,10},{10,... | collective-permute-start | bytes 184328 | tf_op jit(solution)/shard_map/ppermute | solution.py:551
  20.8 1.7 %collective-permute-start.7 = (bf16[240,128]{1,0:T(8,128)(2,1)S(1)}, bf16[240,128]{1,0:T(8,128)(2,1)S(1)}, u32[]{:S(2)}, u32[]{:S(2)}) collective-permute-start(bf16[240,128]{1,0:T(8,128)(2,1)S(1)} %add_convert_fusion.2), channel_id=1, source_target_pairs={{0,2},{1,3},{2,0},{3,1},{4,6},{5,7},{6,4},{7,5},{8,10},{9,11},{10,... | collective-permute-start | bytes 184328 | tf_op jit(solution)/shard_map/ppermute | solution.py:551
  22.5 1.5 %collective-permute-start.6 = (bf16[240,128]{1,0:T(8,128)(2,1)S(1)}, bf16[240,128]{1,0:T(8,128)(2,1)S(1)}, u32[]{:S(2)}, u32[]{:S(2)}) collective-permute-start(bf16[240,128]{1,0:T(8,128)(2,1)S(1)} %add_convert_fusion.2), channel_id=1, source_target_pairs={{0,1},{1,0},{2,3},{3,2},{4,5},{5,4},{6,7},{7,6},{8,9},{9,8},{10,11... | collective-permute-start | bytes 184328 | tf_op jit(solution)/shard_map/ppermute | solution.py:551
  24.0 1.0 %shard_map.78 = bf16[64,256]{1,0:T(8,128)(2,1)} custom-call(f32[17,64,128]{2,1,0:T(8,128)S(1)} %get-tuple-element.39.act_second_ref, bf16[128,128]{1,0:T(8,128)(2,1)S(1)} %get-tuple-element.40.pool_second_ref), custom_call_target="tpu_custom_call" | custom-call | tf_op jit(solution)/shard_map/pallas_call | solution.py:642
  25.0 1.3 %collective-permute-done.8 = bf16[240,128]{1,0:T(8,128)(2,1)S(1)} collective-permute-done((bf16[240,128]{1,0:T(8,128)(2,1)S(1)}, bf16[240,128]{1,0:T(8,128)(2,1)S(1)}, u32[]{:S(2)}, u32[]{:S(2)}) %collective-permute-start.8) | collective-permute-done | bytes 61472 | tf_op jit(solution)/shard_map/ppermute | solution.py:551
  26.3 2.3 %collective-permute-done.7 = bf16[240,128]{1,0:T(8,128)(2,1)S(1)} collective-permute-done((bf16[240,128]{1,0:T(8,128)(2,1)S(1)}, bf16[240,128]{1,0:T(8,128)(2,1)S(1)}, u32[]{:S(2)}, u32[]{:S(2)}) %collective-permute-start.7) | collective-permute-done | bytes 61472 | tf_op jit(solution)/shard_map/ppermute | solution.py:551
  28.7 2.5 %collective-permute-start.11 = (bf16[240,128]{1,0:T(8,128)(2,1)S(1)}, bf16[240,128]{1,0:T(8,128)(2,1)S(1)}, u32[]{:S(2)}, u32[]{:S(2)}) collective-permute-start(bf16[240,128]{1,0:T(8,128)(2,1)S(1)} %add_convert_fusion.1), channel_id=1, source_target_pairs={{0,24},{8,16},{16,8},{24,0},{1,25},{9,17},{17,9},{25,1},{2,26},{10... | collective-permute-start | bytes 184328 | tf_op jit(solution)/shard_map/ppermute | solution.py:551
  31.2 0.5 %collective-permute-start.10 = (bf16[240,128]{1,0:T(8,128)(2,1)S(1)}, bf16[240,128]{1,0:T(8,128)(2,1)S(1)}, u32[]{:S(2)}, u32[]{:S(2)}) collective-permute-start(bf16[240,128]{1,0:T(8,128)(2,1)S(1)} %add_convert_fusion.1), channel_id=1, source_target_pairs={{0,16},{8,24},{16,0},{24,8},{1,17},{9,25},{17,1},{25,9},{2,18},{10... | collective-permute-start | bytes 184328 | tf_op jit(solution)/shard_map/ppermute | solution.py:551
  31.7 0.5 %collective-permute-start.9 = (bf16[240,128]{1,0:T(8,128)(2,1)S(1)}, bf16[240,128]{1,0:T(8,128)(2,1)S(1)}, u32[]{:S(2)}, u32[]{:S(2)}) collective-permute-start(bf16[240,128]{1,0:T(8,128)(2,1)S(1)} %add_convert_fusion.1), channel_id=1, source_target_pairs={{0,8},{8,0},{16,24},{24,16},{1,9},{9,1},{17,25},{25,17},{2,10},{10... | collective-permute-start | bytes 184328 | tf_op jit(solution)/shard_map/ppermute | solution.py:551
  32.2 1.7 %collective-permute-done.11 = bf16[240,128]{1,0:T(8,128)(2,1)S(1)} collective-permute-done((bf16[240,128]{1,0:T(8,128)(2,1)S(1)}, bf16[240,128]{1,0:T(8,128)(2,1)S(1)}, u32[]{:S(2)}, u32[]{:S(2)}) %collective-permute-start.11) | collective-permute-done | bytes 61472 | tf_op jit(solution)/shard_map/ppermute | solution.py:551
  34.0 1.4 %collective-permute-done.10 = bf16[240,128]{1,0:T(8,128)(2,1)S(1)} collective-permute-done((bf16[240,128]{1,0:T(8,128)(2,1)S(1)}, bf16[240,128]{1,0:T(8,128)(2,1)S(1)}, u32[]{:S(2)}, u32[]{:S(2)}) %collective-permute-start.10) | collective-permute-done | bytes 61472 | tf_op jit(solution)/shard_map/ppermute | solution.py:551
  35.4 0.5 %collective-permute-done.9 = bf16[240,128]{1,0:T(8,128)(2,1)S(1)} collective-permute-done((bf16[240,128]{1,0:T(8,128)(2,1)S(1)}, bf16[240,128]{1,0:T(8,128)(2,1)S(1)}, u32[]{:S(2)}, u32[]{:S(2)}) %collective-permute-start.9) | collective-permute-done | bytes 61472 | tf_op jit(solution)/shard_map/ppermute | solution.py:551
  36.0 0.7 %copy.9 = f32[1,32,1,1,2048]{4,3,2,1,0:T(1,128)} copy(f32[1,32,1,1,2048]{4,3,2,1,0:T(1,128)S(1)} %bitcast.17) | data formatting | bytes 524288
  36.8 0.5 %collective-permute-done.12.other_ref = bf16[240,128]{1,0:T(8,128)(2,1)S(1)} collective-permute-done((bf16[240,128]{1,0:T(8,128)(2,1)S(1)}, bf16[240,128]{1,0:T(8,128)(2,1)S(1)}, u32[]{:S(2)}, u32[]{:S(2)}) %collective-permute-start.12) | collective-permute-done | bytes 61472 | tf_op jit(solution)/shard_map/ppermute | solution.py:547
  37.3 0.9 %shard_map.79 = (f32[3,288,64]{2,1,0:T(8,128)}, f32[27,4,32]{2,1,0:T(4,128)}) custom-call(bf16[240,128]{1,0:T(8,128)(2,1)S(1)} %add_convert_fusion.mine_ref, bf16[240,128]{1,0:T(8,128)(2,1)S(1)} %collective-permute-done.12.other_ref), custom_call_target="tpu_custom_call" | custom-call | tf_op jit(solution)/shard_map/pallas_call | solution.py:647
  (13 shorter events, 0.3 us)
Async XLA Ops:
  1.9 8.1 %collective-permute-start = (bf16[48,512]{1,0:T(8,128)(2,1)S(1)}, bf16[48,512]{1,0:T(8,128)(2,1)S(1)}, u32[]{:S(2)}, u32[]{:S(2)}) collective-permute-start(bf16[48,512]{1,0:T(8,128)(2,1)S(1)} %get-tuple-element.26), channel_id=1, source_target_pairs={{0,4},{4,0},{1,5},{5,1},{2,6},{6,2},{3,7},{7,3},{8,12},{12,8},{9,1... | collective-permute-start | bytes 147464 | tf_op jit(solution)/shard_map/ppermute | solution.py:602
  2.4 7.6 %collective-permute-start.1 = (bf16[160,128]{1,0:T(8,128)(2,1)S(1)}, bf16[160,128]{1,0:T(8,128)(2,1)S(1)}, u32[]{:S(2)}, u32[]{:S(2)}) collective-permute-start(bf16[160,128]{1,0:T(8,128)(2,1)S(1)} %get-tuple-element.27), channel_id=1, source_target_pairs={{0,1},{1,0},{2,3},{3,2},{4,5},{5,4},{6,7},{7,6},{8,9},{9,8},{10,11... | collective-permute-start | bytes 122888 | tf_op jit(solution)/shard_map/ppermute | solution.py:600
  5.1 4.9 %collective-permute-start.2 = (bf16[160,128]{1,0:T(8,128)(2,1)S(1)}, bf16[160,128]{1,0:T(8,128)(2,1)S(1)}, u32[]{:S(2)}, u32[]{:S(2)}) collective-permute-start(bf16[160,128]{1,0:T(8,128)(2,1)S(1)} %get-tuple-element.28), channel_id=1, source_target_pairs={{0,4},{1,2},{2,1},{3,7},{4,0},{5,6},{6,5},{7,3},{8,12},{9,10},{10,... | collective-permute-start | bytes 122888 | tf_op jit(solution)/shard_map/ppermute | solution.py:592
  5.2 4.7 %collective-permute-start.3 = (bf16[48,128]{1,0:T(8,128)(2,1)S(1)}, bf16[48,128]{1,0:T(8,128)(2,1)S(1)}, u32[]{:S(2)}, u32[]{:S(2)}) collective-permute-start(bf16[48,128]{1,0:T(8,128)(2,1)S(1)} %get-tuple-element.29), channel_id=1, source_target_pairs={{0,5},{1,4},{2,7},{3,6},{4,1},{5,0},{6,3},{7,2},{8,13},{9,12},{10,... | collective-permute-start | bytes 36872 | tf_op jit(solution)/shard_map/ppermute | solution.py:592
  7.7 2.3 %collective-permute-start.4 = (bf16[48,128]{1,0:T(8,128)(2,1)S(1)}, bf16[48,128]{1,0:T(8,128)(2,1)S(1)}, u32[]{:S(2)}, u32[]{:S(2)}) collective-permute-start(bf16[48,128]{1,0:T(8,128)(2,1)S(1)} %get-tuple-element.30.after_ref), channel_id=1, source_target_pairs={{0,4},{1,6},{2,5},{3,7},{4,0},{5,2},{6,1},{7,3},{8,12},{9,14},{10,... | collective-permute-start | bytes 36872 | tf_op jit(solution)/shard_map/ppermute | solution.py:592
  8.3 1.7 %copy-start = (bf16[1,64,1,1,256]{4,1,3,2,0:T(8,128)(2,1)S(1)}, bf16[1,64,1,1,256]{4,1,3,2,0:T(8,128)(2,1)}, u32[]{:S(2)}) copy-start(bf16[1,64,1,1,256]{4,1,3,2,0:T(8,128)(2,1)} %param.7) | copy-start | bytes 98308
  18.2 1.3 %collective-permute-start.5 = (bf16[240,128]{1,0:T(8,128)(2,1)S(1)}, bf16[240,128]{1,0:T(8,128)(2,1)S(1)}, u32[]{:S(2)}, u32[]{:S(2)}) collective-permute-start(bf16[240,128]{1,0:T(8,128)(2,1)S(1)} %get-tuple-element.38), channel_id=1, source_target_pairs={{0,4},{4,0},{1,5},{5,1},{2,6},{6,2},{3,7},{7,3},{8,12},{12,8},{9,1... | collective-permute-start | bytes 184328 | tf_op jit(solution)/shard_map/ppermute | solution.py:547
  19.5 6.8 %collective-permute-start.8 = (bf16[240,128]{1,0:T(8,128)(2,1)S(1)}, bf16[240,128]{1,0:T(8,128)(2,1)S(1)}, u32[]{:S(2)}, u32[]{:S(2)}) collective-permute-start(bf16[240,128]{1,0:T(8,128)(2,1)S(1)} %add_convert_fusion.2), channel_id=1, source_target_pairs={{0,3},{1,2},{2,1},{3,0},{4,7},{5,6},{6,5},{7,4},{8,11},{9,10},{10,... | collective-permute-start | bytes 184328 | tf_op jit(solution)/shard_map/ppermute | solution.py:551
  20.8 7.8 %collective-permute-start.7 = (bf16[240,128]{1,0:T(8,128)(2,1)S(1)}, bf16[240,128]{1,0:T(8,128)(2,1)S(1)}, u32[]{:S(2)}, u32[]{:S(2)}) collective-permute-start(bf16[240,128]{1,0:T(8,128)(2,1)S(1)} %add_convert_fusion.2), channel_id=1, source_target_pairs={{0,2},{1,3},{2,0},{3,1},{4,6},{5,7},{6,4},{7,5},{8,10},{9,11},{10,... | collective-permute-start | bytes 184328 | tf_op jit(solution)/shard_map/ppermute | solution.py:551
  22.5 6.1 %collective-permute-start.6 = (bf16[240,128]{1,0:T(8,128)(2,1)S(1)}, bf16[240,128]{1,0:T(8,128)(2,1)S(1)}, u32[]{:S(2)}, u32[]{:S(2)}) collective-permute-start(bf16[240,128]{1,0:T(8,128)(2,1)S(1)} %add_convert_fusion.2), channel_id=1, source_target_pairs={{0,1},{1,0},{2,3},{3,2},{4,5},{5,4},{6,7},{7,6},{8,9},{9,8},{10,11... | collective-permute-start | bytes 184328 | tf_op jit(solution)/shard_map/ppermute | solution.py:551
  28.7 5.3 %collective-permute-start.11 = (bf16[240,128]{1,0:T(8,128)(2,1)S(1)}, bf16[240,128]{1,0:T(8,128)(2,1)S(1)}, u32[]{:S(2)}, u32[]{:S(2)}) collective-permute-start(bf16[240,128]{1,0:T(8,128)(2,1)S(1)} %add_convert_fusion.1), channel_id=1, source_target_pairs={{0,24},{8,16},{16,8},{24,0},{1,25},{9,17},{17,9},{25,1},{2,26},{10... | collective-permute-start | bytes 184328 | tf_op jit(solution)/shard_map/ppermute | solution.py:551
  31.2 4.2 %collective-permute-start.10 = (bf16[240,128]{1,0:T(8,128)(2,1)S(1)}, bf16[240,128]{1,0:T(8,128)(2,1)S(1)}, u32[]{:S(2)}, u32[]{:S(2)}) collective-permute-start(bf16[240,128]{1,0:T(8,128)(2,1)S(1)} %add_convert_fusion.1), channel_id=1, source_target_pairs={{0,16},{8,24},{16,0},{24,8},{1,17},{9,25},{17,1},{25,9},{2,18},{10... | collective-permute-start | bytes 184328 | tf_op jit(solution)/shard_map/ppermute | solution.py:551
  31.7 4.2 %collective-permute-start.9 = (bf16[240,128]{1,0:T(8,128)(2,1)S(1)}, bf16[240,128]{1,0:T(8,128)(2,1)S(1)}, u32[]{:S(2)}, u32[]{:S(2)}) collective-permute-start(bf16[240,128]{1,0:T(8,128)(2,1)S(1)} %add_convert_fusion.1), channel_id=1, source_target_pairs={{0,8},{8,0},{16,24},{24,16},{1,9},{9,1},{17,25},{25,17},{2,10},{10... | collective-permute-start | bytes 184328 | tf_op jit(solution)/shard_map/ppermute | solution.py:551
  36.0 1.3 %collective-permute-start.12 = (bf16[240,128]{1,0:T(8,128)(2,1)S(1)}, bf16[240,128]{1,0:T(8,128)(2,1)S(1)}, u32[]{:S(2)}, u32[]{:S(2)}) collective-permute-start(bf16[240,128]{1,0:T(8,128)(2,1)S(1)} %add_convert_fusion.mine_ref), channel_id=1, source_target_pairs={{0,4},{4,0},{1,5},{5,1},{2,6},{6,2},{3,7},{7,3},{8,12},{12,8},{9,1... | collective-permute-start | bytes 184328 | tf_op jit(solution)/shard_map/ppermute | solution.py:547

commit v4 on v2

--- a/solution.py
+++ b/solution.py
@@ -433,12 +433,13 @@
             half_grad[base + m] = split(plane)
 
     def four_first(step):
-        spread = dot(
-            half_grad[4 * step : 4 * step + 4].reshape(256, MID), spread_first_ref[...]
-        )
         backs = []
         for k in range(4):
-            whole = spread[k * 64 : k * 64 + 32] + spread[k * 64 + 32 : k * 64 + 64]
+            if k % 2 == 0:
+                two = half_grad[4 * step + k : 4 * step + k + 2].reshape(128, MID)
+                spread = dot(two, spread_first_ref[...])
+            row = k % 2 * 64
+            whole = spread[row : row + 32] + spread[row + 32 : row + 64]
             less = SLOPE * whole
             pre = pre_first[4 * step + k + 2 * gx]
             parts = [jnp.where(pre[r : r + 32] > 0, whole, less) for r in (0, 32)]

time: 37 us -> 37 us (level)
  no operation moved by 1% of the time
where the time goes in v4:
time: 37 us; the launch traced here: 36.8 us
  starting transfers between devices  14.6 us (39%)
  Pallas kernels  13 us (35%)
  waiting for transfers between devices  7.68 us (21%)
  between operations  0.73 us (2%)
  local copies, waits for them, and re-layouts  0.71 us (2%)
    pallas_call x1, Pallas kernels, on_device_kernels(): call(functools.partial(main_kernel, rows_y), [((NS, 64, MID), F32), ((32,...  8.2 us
    ppermute x6, starting transfers between devices, sum_of_four(): lax.ppermute(part, axis, [(i, i ^ k) for i in range(4)])  8.01 us
    ppermute x6, waiting for transfers between devices, sum_of_four(): lax.ppermute(part, axis, [(i, i ^ k) for i in range(4)])  5.96 us
    ppermute x3, starting transfers between devices, paired(): return lax.ppermute(values, ('gx', 'yz'), routes)  3.27 us
    ppermute x1, starting transfers between devices, on_device_kernels(): got_near = lax.ppermute(near, 'yz', [(i, i ^ 1) for i in range(rows_y)])  2.65 us
    ppermute x2, waiting for transfers between devices, swap_cores(): return lax.ppermute(values, 'gx', [(0, 1), (1, 0)])  1.71 us
    pallas_call x1, Pallas kernels, on_device_kernels(): call(prepare_kernel, [((64, 144), BF16), ((256, 1728), BF16), ((128, 3456...  1.61 us
    pallas_call x1, Pallas kernels, on_device_kernels(): call(pack_kernel, [((136, OWN), F32), ((48, OWN), BF16), ((160, 128), BF1...  1.26 us
  transfers between devices with their start and end apart: 13, of which 8 were waited for; matrix products, arithmetic and copies ran while one was open for 2% of the time, Pallas kernels for 7%

profile of v4, /device:TPU:0, one launch (start us, length us, event | category | flops | bytes accessed | tf_op | source)
XLA Modules:
  0.0 36.8 jit_solution(16274473827897078645)
XLA Ops:
  0.6 1.3 %shard_map.75 = (f32[136,512]{1,0:T(8,128)S(1)}, bf16[48,512]{1,0:T(8,128)(2,1)S(1)}, bf16[160,128]{1,0:T(8,128)(2,1)S(1)}, bf16[160,128]{1,0:T(8,128)(2,1)S(1)}...) custom-call(bf16[4,16384]{1,0:T(4,128)(2,1)} %bitcast.21, bf16[64,256]{1,0:T(8,128)(2,1)} %bitcast.19), custom_call_target="tpu_custom_call" | custom-call | tf_op jit(solution)/shard_map/pallas_call | solution.py:561
  1.9 0.5 %collective-permute-start = (bf16[48,512]{1,0:T(8,128)(2,1)S(1)}, bf16[48,512]{1,0:T(8,128)(2,1)S(1)}, u32[]{:S(2)}, u32[]{:S(2)}) collective-permute-start(bf16[48,512]{1,0:T(8,128)(2,1)S(1)} %get-tuple-element.26), channel_id=1, source_target_pairs={{0,4},{4,0},{1,5},{5,1},{2,6},{6,2},{3,7},{7,3},{8,12},{12,8},{9,1... | collective-permute-start | bytes 147464 | tf_op jit(solution)/shard_map/ppermute | solution.py:603
  2.4 2.7 %collective-permute-start.1 = (bf16[160,128]{1,0:T(8,128)(2,1)S(1)}, bf16[160,128]{1,0:T(8,128)(2,1)S(1)}, u32[]{:S(2)}, u32[]{:S(2)}) collective-permute-start(bf16[160,128]{1,0:T(8,128)(2,1)S(1)} %get-tuple-element.27), channel_id=1, source_target_pairs={{0,1},{1,0},{2,3},{3,2},{4,5},{5,4},{6,7},{7,6},{8,9},{9,8},{10,11... | collective-permute-start | bytes 122888 | tf_op jit(solution)/shard_map/ppermute | solution.py:601
  5.1 0.2 collective-permute-start.2
  5.2 2.5 %collective-permute-start.3 = (bf16[48,128]{1,0:T(8,128)(2,1)S(1)}, bf16[48,128]{1,0:T(8,128)(2,1)S(1)}, u32[]{:S(2)}, u32[]{:S(2)}) collective-permute-start(bf16[48,128]{1,0:T(8,128)(2,1)S(1)} %get-tuple-element.29), channel_id=1, source_target_pairs={{0,5},{1,4},{2,7},{3,6},{4,1},{5,0},{6,3},{7,2},{8,13},{9,12},{10,... | collective-permute-start | bytes 36872 | tf_op jit(solution)/shard_map/ppermute | solution.py:593
  7.7 0.6 %collective-permute-start.4 = (bf16[48,128]{1,0:T(8,128)(2,1)S(1)}, bf16[48,128]{1,0:T(8,128)(2,1)S(1)}, u32[]{:S(2)}, u32[]{:S(2)}) collective-permute-start(bf16[48,128]{1,0:T(8,128)(2,1)S(1)} %get-tuple-element.30.after_ref), channel_id=1, source_target_pairs={{0,4},{1,6},{2,5},{3,7},{4,0},{5,2},{6,1},{7,3},{8,12},{9,14},{10,... | collective-permute-start | bytes 36872 | tf_op jit(solution)/shard_map/ppermute | solution.py:593
  8.3 1.6 %shard_map.76 = (bf16[64,144]{1,0:T(8,128)(2,1)S(1)}, bf16[256,1728]{1,0:T(8,128)(2,1)S(1)}, bf16[128,3456]{1,0:T(8,128)(2,1)S(1)}, bf16[640,256]{1,0:T(8,128)(2...) custom-call(bf16[48,128]{1,0:T(8,128)(2,1)S(1)} %get-tuple-element.30.after_ref, ...), custom_call_target="tpu_custom_call" | custom-call | flops 100000000 | bytes 2000000 | tf_op jit(solution)/shard_map/pallas_call | solution.py:573
  10.0 8.2 %shard_map.77 = (f32[17,64,128]{2,1,0:T(8,128)S(1)}, f32[32,16,128]{2,1,0:T(8,128)S(1)}, f32[240,128]{1,0:T(8,128)S(1)}, bf16[240,128]{1,0:T(8,128)(2,1)S(1)}) custom-call(f32[17,8,512]{2,1,0:T(8,128)S(1)} %bitcast.18, bf16[64,256]{1,0:T(8,128)(2,1)S(1)} %bitcast.20, bf16[48,512]{1,0:T(8,128)(2,1)S(1)} %collective-permute-done.rx_ref, ...), custom_call_target="tpu_custom_call" | custom-call | tf_op jit(solution)/shard_map/pallas_call | solution.py:607
  18.4 1.2 %collective-permute-done.5 = bf16[240,128]{1,0:T(8,128)(2,1)S(1)} collective-permute-done((bf16[240,128]{1,0:T(8,128)(2,1)S(1)}, bf16[240,128]{1,0:T(8,128)(2,1)S(1)}, u32[]{:S(2)}, u32[]{:S(2)}) %collective-permute-start.5) | collective-permute-done | bytes 61472 | tf_op jit(solution)/shard_map/ppermute | solution.py:548
  19.6 2.5 %collective-permute-start.8 = (bf16[240,128]{1,0:T(8,128)(2,1)S(1)}, bf16[240,128]{1,0:T(8,128)(2,1)S(1)}, u32[]{:S(2)}, u32[]{:S(2)}) collective-permute-start(bf16[240,128]{1,0:T(8,128)(2,1)S(1)} %add_convert_fusion.2), channel_id=1, source_target_pairs={{0,24},{8,16},{16,8},{24,0},{1,25},{9,17},{17,9},{25,1},{2,26},{10... | collective-permute-start | bytes 184328 | tf_op jit(solution)/shard_map/ppermute | solution.py:552
  22.1 0.5 %collective-permute-start.7 = (bf16[240,128]{1,0:T(8,128)(2,1)S(1)}, bf16[240,128]{1,0:T(8,128)(2,1)S(1)}, u32[]{:S(2)}, u32[]{:S(2)}) collective-permute-start(bf16[240,128]{1,0:T(8,128)(2,1)S(1)} %add_convert_fusion.2), channel_id=1, source_target_pairs={{0,16},{8,24},{16,0},{24,8},{1,17},{9,25},{17,1},{25,9},{2,18},{10... | collective-permute-start | bytes 184328 | tf_op jit(solution)/shard_map/ppermute | solution.py:552
  22.6 0.5 %collective-permute-start.6 = (bf16[240,128]{1,0:T(8,128)(2,1)S(1)}, bf16[240,128]{1,0:T(8,128)(2,1)S(1)}, u32[]{:S(2)}, u32[]{:S(2)}) collective-permute-start(bf16[240,128]{1,0:T(8,128)(2,1)S(1)} %add_convert_fusion.2), channel_id=1, source_target_pairs={{0,8},{8,0},{16,24},{24,16},{1,9},{9,1},{17,25},{25,17},{2,10},{10... | collective-permute-start | bytes 184328 | tf_op jit(solution)/shard_map/ppermute | solution.py:552
  23.1 1.0 %shard_map.78 = bf16[64,256]{1,0:T(8,128)(2,1)} custom-call(f32[17,64,128]{2,1,0:T(8,128)S(1)} %get-tuple-element.39.act_second_ref, bf16[128,128]{1,0:T(8,128)(2,1)S(1)} %get-tuple-element.40.pool_second_ref), custom_call_target="tpu_custom_call" | custom-call | tf_op jit(solution)/shard_map/pallas_call | solution.py:643
  24.1 0.6 %collective-permute-done.8 = bf16[240,128]{1,0:T(8,128)(2,1)S(1)} collective-permute-done((bf16[240,128]{1,0:T(8,128)(2,1)S(1)}, bf16[240,128]{1,0:T(8,128)(2,1)S(1)}, u32[]{:S(2)}, u32[]{:S(2)}) %collective-permute-start.8) | collective-permute-done | bytes 61472 | tf_op jit(solution)/shard_map/ppermute | solution.py:552
  24.8 1.5 %collective-permute-done.7 = bf16[240,128]{1,0:T(8,128)(2,1)S(1)} collective-permute-done((bf16[240,128]{1,0:T(8,128)(2,1)S(1)}, bf16[240,128]{1,0:T(8,128)(2,1)S(1)}, u32[]{:S(2)}, u32[]{:S(2)}) %collective-permute-start.7) | collective-permute-done | bytes 61472 | tf_op jit(solution)/shard_map/ppermute | solution.py:552
  26.3 0.5 %collective-permute-done.6 = bf16[240,128]{1,0:T(8,128)(2,1)S(1)} collective-permute-done((bf16[240,128]{1,0:T(8,128)(2,1)S(1)}, bf16[240,128]{1,0:T(8,128)(2,1)S(1)}, u32[]{:S(2)}, u32[]{:S(2)}) %collective-permute-start.6) | collective-permute-done | bytes 61472 | tf_op jit(solution)/shard_map/ppermute | solution.py:552
  26.8 1.3 %collective-permute-start.11 = (bf16[240,128]{1,0:T(8,128)(2,1)S(1)}, bf16[240,128]{1,0:T(8,128)(2,1)S(1)}, u32[]{:S(2)}, u32[]{:S(2)}) collective-permute-start(bf16[240,128]{1,0:T(8,128)(2,1)S(1)} %add_convert_fusion.1), channel_id=1, source_target_pairs={{0,3},{1,2},{2,1},{3,0},{4,7},{5,6},{6,5},{7,4},{8,11},{9,10},{10,... | collective-permute-start | bytes 184328 | tf_op jit(solution)/shard_map/ppermute | solution.py:552
  28.1 1.7 %collective-permute-start.10 = (bf16[240,128]{1,0:T(8,128)(2,1)S(1)}, bf16[240,128]{1,0:T(8,128)(2,1)S(1)}, u32[]{:S(2)}, u32[]{:S(2)}) collective-permute-start(bf16[240,128]{1,0:T(8,128)(2,1)S(1)} %add_convert_fusion.1), channel_id=1, source_target_pairs={{0,2},{1,3},{2,0},{3,1},{4,6},{5,7},{6,4},{7,5},{8,10},{9,11},{10,... | collective-permute-start | bytes 184328 | tf_op jit(solution)/shard_map/ppermute | solution.py:552
  29.8 1.5 %collective-permute-start.9 = (bf16[240,128]{1,0:T(8,128)(2,1)S(1)}, bf16[240,128]{1,0:T(8,128)(2,1)S(1)}, u32[]{:S(2)}, u32[]{:S(2)}) collective-permute-start(bf16[240,128]{1,0:T(8,128)(2,1)S(1)} %add_convert_fusion.1), channel_id=1, source_target_pairs={{0,1},{1,0},{2,3},{3,2},{4,5},{5,4},{6,7},{7,6},{8,9},{9,8},{10,11... | collective-permute-start | bytes 184328 | tf_op jit(solution)/shard_map/ppermute | solution.py:552
  31.3 1.7 %collective-permute-done.11 = bf16[240,128]{1,0:T(8,128)(2,1)S(1)} collective-permute-done((bf16[240,128]{1,0:T(8,128)(2,1)S(1)}, bf16[240,128]{1,0:T(8,128)(2,1)S(1)}, u32[]{:S(2)}, u32[]{:S(2)}) %collective-permute-start.11) | collective-permute-done | bytes 61472 | tf_op jit(solution)/shard_map/ppermute | solution.py:552
  33.0 1.5 %collective-permute-done.10 = bf16[240,128]{1,0:T(8,128)(2,1)S(1)} collective-permute-done((bf16[240,128]{1,0:T(8,128)(2,1)S(1)}, bf16[240,128]{1,0:T(8,128)(2,1)S(1)}, u32[]{:S(2)}, u32[]{:S(2)}) %collective-permute-start.10) | collective-permute-done | bytes 61472 | tf_op jit(solution)/shard_map/ppermute | solution.py:552
  34.7 0.7 %copy.9 = f32[1,32,1,1,2048]{4,3,2,1,0:T(1,128)} copy(f32[1,32,1,1,2048]{4,3,2,1,0:T(1,128)S(1)} %bitcast.17) | data formatting | bytes 524288
  35.4 0.5 %collective-permute-done.12.other_ref = bf16[240,128]{1,0:T(8,128)(2,1)S(1)} collective-permute-done((bf16[240,128]{1,0:T(8,128)(2,1)S(1)}, bf16[240,128]{1,0:T(8,128)(2,1)S(1)}, u32[]{:S(2)}, u32[]{:S(2)}) %collective-permute-start.12) | collective-permute-done | bytes 61472 | tf_op jit(solution)/shard_map/ppermute | solution.py:548
  36.0 0.9 %shard_map.79 = (f32[3,288,64]{2,1,0:T(8,128)}, f32[27,4,32]{2,1,0:T(4,128)}) custom-call(bf16[240,128]{1,0:T(8,128)(2,1)S(1)} %add_convert_fusion.mine_ref, bf16[240,128]{1,0:T(8,128)(2,1)S(1)} %collective-permute-done.12.other_ref), custom_call_target="tpu_custom_call" | custom-call | tf_op jit(solution)/shard_map/pallas_call | solution.py:648
  (13 shorter events, 0.4 us)
Async XLA Ops:
  1.9 8.1 %collective-permute-start = (bf16[48,512]{1,0:T(8,128)(2,1)S(1)}, bf16[48,512]{1,0:T(8,128)(2,1)S(1)}, u32[]{:S(2)}, u32[]{:S(2)}) collective-permute-start(bf16[48,512]{1,0:T(8,128)(2,1)S(1)} %get-tuple-element.26), channel_id=1, source_target_pairs={{0,4},{4,0},{1,5},{5,1},{2,6},{6,2},{3,7},{7,3},{8,12},{12,8},{9,1... | collective-permute-start | bytes 147464 | tf_op jit(solution)/shard_map/ppermute | solution.py:603
  2.4 7.6 %collective-permute-start.1 = (bf16[160,128]{1,0:T(8,128)(2,1)S(1)}, bf16[160,128]{1,0:T(8,128)(2,1)S(1)}, u32[]{:S(2)}, u32[]{:S(2)}) collective-permute-start(bf16[160,128]{1,0:T(8,128)(2,1)S(1)} %get-tuple-element.27), channel_id=1, source_target_pairs={{0,1},{1,0},{2,3},{3,2},{4,5},{5,4},{6,7},{7,6},{8,9},{9,8},{10,11... | collective-permute-start | bytes 122888 | tf_op jit(solution)/shard_map/ppermute | solution.py:601
  5.1 4.9 %collective-permute-start.2 = (bf16[160,128]{1,0:T(8,128)(2,1)S(1)}, bf16[160,128]{1,0:T(8,128)(2,1)S(1)}, u32[]{:S(2)}, u32[]{:S(2)}) collective-permute-start(bf16[160,128]{1,0:T(8,128)(2,1)S(1)} %get-tuple-element.28), channel_id=1, source_target_pairs={{0,4},{1,2},{2,1},{3,7},{4,0},{5,6},{6,5},{7,3},{8,12},{9,10},{10,... | collective-permute-start | bytes 122888 | tf_op jit(solution)/shard_map/ppermute | solution.py:593
  5.2 4.7 %collective-permute-start.3 = (bf16[48,128]{1,0:T(8,128)(2,1)S(1)}, bf16[48,128]{1,0:T(8,128)(2,1)S(1)}, u32[]{:S(2)}, u32[]{:S(2)}) collective-permute-start(bf16[48,128]{1,0:T(8,128)(2,1)S(1)} %get-tuple-element.29), channel_id=1, source_target_pairs={{0,5},{1,4},{2,7},{3,6},{4,1},{5,0},{6,3},{7,2},{8,13},{9,12},{10,... | collective-permute-start | bytes 36872 | tf_op jit(solution)/shard_map/ppermute | solution.py:593
  7.7 2.3 %collective-permute-start.4 = (bf16[48,128]{1,0:T(8,128)(2,1)S(1)}, bf16[48,128]{1,0:T(8,128)(2,1)S(1)}, u32[]{:S(2)}, u32[]{:S(2)}) collective-permute-start(bf16[48,128]{1,0:T(8,128)(2,1)S(1)} %get-tuple-element.30.after_ref), channel_id=1, source_target_pairs={{0,4},{1,6},{2,5},{3,7},{4,0},{5,2},{6,1},{7,3},{8,12},{9,14},{10,... | collective-permute-start | bytes 36872 | tf_op jit(solution)/shard_map/ppermute | solution.py:593
  8.3 1.7 %copy-start = (bf16[1,64,1,1,256]{4,1,3,2,0:T(8,128)(2,1)S(1)}, bf16[1,64,1,1,256]{4,1,3,2,0:T(8,128)(2,1)}, u32[]{:S(2)}) copy-start(bf16[1,64,1,1,256]{4,1,3,2,0:T(8,128)(2,1)} %param.7) | copy-start | bytes 98308
  18.2 1.3 %collective-permute-start.5 = (bf16[240,128]{1,0:T(8,128)(2,1)S(1)}, bf16[240,128]{1,0:T(8,128)(2,1)S(1)}, u32[]{:S(2)}, u32[]{:S(2)}) collective-permute-start(bf16[240,128]{1,0:T(8,128)(2,1)S(1)} %get-tuple-element.38), channel_id=1, source_target_pairs={{0,4},{4,0},{1,5},{5,1},{2,6},{6,2},{3,7},{7,3},{8,12},{12,8},{9,1... | collective-permute-start | bytes 184328 | tf_op jit(solution)/shard_map/ppermute | solution.py:548
  19.6 5.2 %collective-permute-start.8 = (bf16[240,128]{1,0:T(8,128)(2,1)S(1)}, bf16[240,128]{1,0:T(8,128)(2,1)S(1)}, u32[]{:S(2)}, u32[]{:S(2)}) collective-permute-start(bf16[240,128]{1,0:T(8,128)(2,1)S(1)} %add_convert_fusion.2), channel_id=1, source_target_pairs={{0,24},{8,16},{16,8},{24,0},{1,25},{9,17},{17,9},{25,1},{2,26},{10... | collective-permute-start | bytes 184328 | tf_op jit(solution)/shard_map/ppermute | solution.py:552
  22.1 4.2 %collective-permute-start.7 = (bf16[240,128]{1,0:T(8,128)(2,1)S(1)}, bf16[240,128]{1,0:T(8,128)(2,1)S(1)}, u32[]{:S(2)}, u32[]{:S(2)}) collective-permute-start(bf16[240,128]{1,0:T(8,128)(2,1)S(1)} %add_convert_fusion.2), channel_id=1, source_target_pairs={{0,16},{8,24},{16,0},{24,8},{1,17},{9,25},{17,1},{25,9},{2,18},{10... | collective-permute-start | bytes 184328 | tf_op jit(solution)/shard_map/ppermute | solution.py:552
  22.6 4.2 %collective-permute-start.6 = (bf16[240,128]{1,0:T(8,128)(2,1)S(1)}, bf16[240,128]{1,0:T(8,128)(2,1)S(1)}, u32[]{:S(2)}, u32[]{:S(2)}) collective-permute-start(bf16[240,128]{1,0:T(8,128)(2,1)S(1)} %add_convert_fusion.2), channel_id=1, source_target_pairs={{0,8},{8,0},{16,24},{24,16},{1,9},{9,1},{17,25},{25,17},{2,10},{10... | collective-permute-start | bytes 184328 | tf_op jit(solution)/shard_map/ppermute | solution.py:552
  26.8 6.2 %collective-permute-start.11 = (bf16[240,128]{1,0:T(8,128)(2,1)S(1)}, bf16[240,128]{1,0:T(8,128)(2,1)S(1)}, u32[]{:S(2)}, u32[]{:S(2)}) collective-permute-start(bf16[240,128]{1,0:T(8,128)(2,1)S(1)} %add_convert_fusion.1), channel_id=1, source_target_pairs={{0,3},{1,2},{2,1},{3,0},{4,7},{5,6},{6,5},{7,4},{8,11},{9,10},{10,... | collective-permute-start | bytes 184328 | tf_op jit(solution)/shard_map/ppermute | solution.py:552
  28.1 6.4 %collective-permute-start.10 = (bf16[240,128]{1,0:T(8,128)(2,1)S(1)}, bf16[240,128]{1,0:T(8,128)(2,1)S(1)}, u32[]{:S(2)}, u32[]{:S(2)}) collective-permute-start(bf16[240,128]{1,0:T(8,128)(2,1)S(1)} %add_convert_fusion.1), channel_id=1, source_target_pairs={{0,2},{1,3},{2,0},{3,1},{4,6},{5,7},{6,4},{7,5},{8,10},{9,11},{10,... | collective-permute-start | bytes 184328 | tf_op jit(solution)/shard_map/ppermute | solution.py:552
  29.8 4.8 %collective-permute-start.9 = (bf16[240,128]{1,0:T(8,128)(2,1)S(1)}, bf16[240,128]{1,0:T(8,128)(2,1)S(1)}, u32[]{:S(2)}, u32[]{:S(2)}) collective-permute-start(bf16[240,128]{1,0:T(8,128)(2,1)S(1)} %add_convert_fusion.1), channel_id=1, source_target_pairs={{0,1},{1,0},{2,3},{3,2},{4,5},{5,4},{6,7},{7,6},{8,9},{9,8},{10,11... | collective-permute-start | bytes 184328 | tf_op jit(solution)/shard_map/ppermute | solution.py:552
  34.6 1.3 %collective-permute-start.12 = (bf16[240,128]{1,0:T(8,128)(2,1)S(1)}, bf16[240,128]{1,0:T(8,128)(2,1)S(1)}, u32[]{:S(2)}, u32[]{:S(2)}) collective-permute-start(bf16[240,128]{1,0:T(8,128)(2,1)S(1)} %add_convert_fusion.mine_ref), channel_id=1, source_target_pairs={{0,4},{4,0},{1,5},{5,1},{2,6},{6,2},{3,7},{7,3},{8,12},{12,8},{9,1... | collective-permute-start | bytes 184328 | tf_op jit(solution)/shard_map/ppermute | solution.py:548
